TPU v7x, 32 devices: a whole 2x2x4 slice. The times are simulated.
32 devices in a mesh: axial: 8 (over z, x), azim: 2 (over y), bank: 2 (over core).
Axes of the slice: x: 2, y: 2, z: 4, core: 2. Of those that a mesh axis runs over, the one named last changes fastest.
Arguments:
- adjoint_state: float32 [2, 64, 64, 512], P('bank', None, 'axial', 'azim'), may hold values from -6 to 6
- adjoint_source: float32 [2, 64, 64, 512], P('bank', None, 'axial', 'azim'), may hold values from -6 to 6
- reaction_rate: float32 [2, 64, 512], P('bank', 'axial', 'azim'), may hold values from 0.5 to 2
- jacobian: float32 [2, 64, 64], P('bank'), may hold values from -0.75 to 0.75
- lifting: float32 [2, 6, 64, 512], P('bank', None, 'axial', 'azim'), may hold values from -0.125 to 0.125
- separator: int32 [8, 2, 2, 6], P('axial', 'azim', 'bank'), may hold values from 0 to 2047
- leaf_schur: float32 [8, 2, 2, 384, 384], P('axial', 'azim', 'bank'), may hold values from -14 to 43, as said below
Outputs:
- interface_adjoint: float32 [8, 2, 2, 384], P('axial', 'azim', 'bank')
Inputs may be any that keep to these rules, and one draw needn't show every extreme that they name: `separator`: a cell k = row * 256 + column of the device's own block. `leaf_schur`: every leaf block is symmetric positive definite.
All inputs are finite; a program needn't handle non-finite values.
Results may differ from a plain program's by a relative error of at most 0.0003.
Values sent between devices are 32-bit elements; how exact they have to be, the bound alone decides.
No kernel may reach another device: no remote copies, remote signals or barrier semaphores. Data moves between devices by JAX's collectives and lax.ppermute only.
A program may use at most 64 MiB of HBM per device.

v0:
```python
import functools

import jax
import jax.numpy as jnp
from jax import lax
from jax.experimental import pallas as pl
from jax.experimental.pallas import tpu as pltpu
from jax.sharding import PartitionSpec as P

highest = lax.Precision.HIGHEST
high = lax.Precision.HIGH
everywhere = ("axial", "azim", "bank")
panel = 64
lanes = 128


def mm(a, b, precision=highest):
    return jnp.dot(a, b, precision=precision, preferred_element_type=jnp.float32)


def mm_nt(a, b, precision=highest):
    dims = (((1,), (1,)), ((), ()))
    return lax.dot_general(a, b, dims, precision=precision, preferred_element_type=jnp.float32)


def sweep_panel(groups, first, forget=False):
    n = len(groups)
    groups = [list(g) for g in groups]
    widths = [t.shape[1] for t in groups[0]]
    row = lax.broadcasted_iota(jnp.int32, (8, lanes), 0)
    lane_of = [lax.broadcasted_iota(jnp.int32, (8, w), 1) for w in widths]
    row_of = [lax.broadcasted_iota(jnp.int32, (8, w), 0) for w in widths]

    def columns(q, s):
        tile, lane = divmod(first + 8 * s, lanes)
        return [jnp.broadcast_to(groups[q][tile][:, lane + m : lane + m + 1], (8, lanes)) for m in range(8)]

    def across(column, tile):
        return column if widths[tile] == lanes else column[:, : widths[tile]]

    def spread(value, i):
        return jnp.broadcast_to(value[i : i + 1], value.shape)

    def inside(s):
        tile, lane = divmod(first + 8 * s, lanes)
        return tile, lane, (lane_of[tile] >= lane) & (lane_of[tile] < lane + 8)

    def update(q, s, cols, solved):
        home, _, here = inside(s)
        new = []
        for k, tile in enumerate(groups[q]):
            if solved[k] is None:
                new.append(tile)
                continue
            value = jnp.where(here, 0.0, tile) if k == home else tile
            for m in range(8):
                value = value - across(cols[m], k) * spread(solved[k], m)
            new.append(value)
        groups[q] = new

    diag = columns(0, 0)
    cols = {q: columns(q, 0) for q in range(1, n)}
    pending = []
    for s in range(n):
        more = s + 1 < n
        if more:
            low, after = list(cols[s + 1]), columns(s + 1, s + 1)
        home, lane, here = inside(s)
        own = list(groups[s])
        live = [k for k in range(len(own)) if not forget or (k + 1) * lanes > first + 8 * s]
        own[home] = jnp.where(here, jnp.where(lane_of[home] - lane == row_of[home], 1.0, 0.0), own[home])
        scale = None
        for p in range(8):
            inverse = 1.0 / spread(diag[p], p)
            scale = inverse if scale is None else jnp.where(row == p, inverse, scale)
            factor = jnp.where(row == p, 0.0, diag[p] * inverse)
            if more:
                low_factor = low[p] * inverse
            for j in range(p + 1, 8):
                entry = spread(diag[j], p)
                diag[j] = diag[j] - factor * entry
                if more:
                    low[j] = low[j] - low_factor * entry
            if more:
                for j in range(8):
                    after[j] = after[j] - low_factor * spread(low[p], j)
            for k in live:
                own[k] = own[k] - across(factor, k) * spread(own[k], p)
            if pending:
                q, *rest = pending.pop(0)
                update(q, *rest)
                cols[q] = columns(q, s)
        solved = [tile * across(scale, k) if k in live else None for k, tile in enumerate(own)]
        groups[s] = [own[k] if tile is None else tile for k, tile in enumerate(solved)]
        for q in list(range(s + 1, n)) + list(range(s)):
            if s < q < s + 3:
                update(q, s, cols[q], solved)
            else:
                pending.append((q, s, cols[q], solved))
        if more:
            diag = after
            cols[s] = columns(s, s + 1)
            if s + 2 < n:
                cols[s + 2] = columns(s + 2, s + 1)
    for work in pending:
        update(*work)
    return groups


def invert(slabs, forget=False):
    slabs = list(slabs)
    n = slabs[0].shape[1]
    lane = lax.broadcasted_iota(jnp.int32, (1, n), 1)
    for p in range(len(slabs)):
        lo = p * panel
        w = slabs[p]
        groups = [[w[i : i + 8, t : min(t + lanes, n)] for t in range(0, n, lanes)] for i in range(0, panel, 8)]
        groups = sweep_panel(groups, lo, forget)
        w = jnp.concatenate([jnp.concatenate(g, axis=1) for g in groups], axis=0)
        slabs[p] = w
        here = (lane >= lo) & (lane < lo + panel)
        for q in list(range(p + 1, len(slabs))) + list(range(p)):
            if forget and p + 1 == len(slabs):
                slabs[q] = slabs[q][:, -lanes:] - mm(slabs[q][:, lo : lo + panel], w[:, -lanes:])
            else:
                slabs[q] = jnp.where(here, 0.0, slabs[q]) - mm(slabs[q][:, lo : lo + panel], w)
    return jnp.concatenate([slab[:, -lanes:] if forget else slab for slab in slabs], axis=0)


def invert_whole(a):
    return invert([a[i : i + panel] for i in range(0, a.shape[0], panel)])


def pack_symmetric(m):
    third = m.shape[0] // 3
    low = jnp.concatenate([m[:third, 2 * third :], m[2 * third :, 2 * third :]], axis=1)
    return jnp.concatenate([m[:third, : 2 * third], m[third : 2 * third, third:], low], axis=0)


def unpack_symmetric(p):
    third = p.shape[0] // 3
    top, mid, low = p[:third], p[third : 2 * third], p[2 * third :]
    return [
        jnp.concatenate([top, low[:, :third]], axis=1),
        jnp.concatenate([top[:, third:].T, mid], axis=1),
        jnp.concatenate([low[:, :third].T, mid[:, third:].T, low[:, third:]], axis=1),
    ]


def pack_full(m):
    half = m.shape[0] // 2
    tail = jnp.concatenate([m[:half, lanes:], m[half:, lanes:]], axis=1)
    return jnp.concatenate([m[:, :lanes], tail], axis=0)


def unpack_full(p):
    n = p.shape[0] * 2 // 3
    tail = p[n:]
    rest = jnp.concatenate([tail[:, : lanes // 2], tail[:, lanes // 2 :]], axis=0)
    return jnp.concatenate([p[:n], rest], axis=1)


def to_row(f):
    return jnp.concatenate([f[i : i + 1] for i in range(3)], axis=1)


def from_row(row):
    parts = [row[:, i * lanes : (i + 1) * lanes] for i in range(3)]
    return jnp.concatenate(parts + [jnp.zeros((5, lanes), jnp.float32)], axis=0)


def leaf_kernel(sep_ref, after_this_ref, state_ref, source_ref, rate_ref, jac_ref, lift_ref, before_ref, after_ref, sides_ref, f_ref):
    seps = sep_ref.shape[1]
    rows = rate_ref.shape[0]
    width = rate_ref.shape[1]
    chans = jac_ref.shape[0]
    lane = lax.broadcasted_iota(jnp.int32, (8, width), 1)
    c_of = lax.broadcasted_iota(jnp.int32, (8, seps), 0)
    own_c = c_of == lax.broadcasted_iota(jnp.int32, (8, seps), 1)
    where = jnp.max(jnp.where(own_c, sep_ref[...], -1), axis=1, keepdims=True)
    lift = []
    for i in range(rows):
        own = lift_ref[:, i, :]
        own = jnp.concatenate([own, jnp.zeros((8 - seps, width), jnp.float32)], axis=0)
        lift.append(own + jnp.where(where == lane + i * width, 1.0, 0.0))
    zero = jnp.zeros((8, width), jnp.float32)
    mixed = []
    for i in range(rows):
        own = lift[i]
        around = (lift[i - 1] if i > 0 else zero) + (lift[i + 1] if i + 1 < rows else zero)
        around = around + jnp.where(lane == 0, 0.0, pltpu.roll(own, 1, 1))
        around = around + jnp.where(lane == width - 1, 0.0, pltpu.roll(own, width - 1, 1))
        mixed.append(jnp.concatenate([0.5 * around - 2.0 * own, own * rate_ref[i : i + 1, :]], axis=0))
    state = jnp.concatenate([state_ref[:, i, :] for i in range(rows)], axis=1)
    source = jnp.concatenate([source_ref[:, i, :] for i in range(rows)], axis=1)
    prod = mm_nt(jnp.concatenate(mixed, axis=1), state, high)
    first = jnp.concatenate([own[:, :1] for own in lift], axis=1)
    last = jnp.concatenate([own[:, width - 1 :] for own in lift], axis=1)
    edge = mm_nt(lift[0], before_ref[...], high) + mm_nt(lift[-1], after_ref[...], high)
    edge = edge + mm_nt(first, sides_ref[chans:, :], high) + mm_nt(last, sides_ref[:chans, :], high)
    total = prod[:8] + mm_nt(jnp.concatenate(lift, axis=1), source, high)
    total = total - mm(prod[8:], jac_ref[...], high) + 0.5 * edge
    out = [jnp.concatenate([total[2 * i : 2 * i + 1], total[2 * i + 1 : 2 * i + 2]], axis=1) for i in range(seps // 2)]
    out.append(jnp.zeros((8 - seps // 2, lanes), jnp.float32))
    f_ref[...] = jnp.concatenate(out, axis=0)


def edges_kernel(state_ref, top_ref, bottom_ref, sides_ref):
    rows, cells = state_ref.shape[1:]
    top_ref[...] = state_ref[:, 0, :]
    bottom_ref[...] = state_ref[:, rows - 1, :]
    left = jnp.concatenate([state_ref[:, i, :1] for i in range(rows)], axis=1)
    right = jnp.concatenate([state_ref[:, i, cells - 1 :] for i in range(rows)], axis=1)
    sides_ref[...] = jnp.concatenate([left, right], axis=0)


def is_upper(level):
    return jnp.bitwise_and(jnp.right_shift(lax.axis_index(everywhere), level), 1) != 0


def order(upper, own, other):
    return jnp.where(upper, other, own), jnp.where(upper, own, other)


def first_kernel(own_ref, other_ref, ss_ref, inv_ref, xt_ref):
    half = own_ref.shape[0] // 2
    upper = is_upper(0)
    inverse = invert_whole(own_ref[half:, half:] + other_ref[half:, half:])
    inv_ref[...] = inverse
    _, os2 = order(upper, own_ref[:half, half:], other_ref[:half, half:])
    _, oo2 = order(upper, own_ref[:half, :half], other_ref[:half, :half])
    xt2 = mm(os2, inverse)
    xt_ref[...] = xt2
    ss_ref[...] = pack_symmetric(oo2 - mm_nt(xt2, os2))


def factor_kernel(own_ref, other_ref, inv_ref):
    inv_ref[...] = invert(unpack_symmetric(own_ref[...] + other_ref[...]))


def shared_kernel(level, inv_ref, own_ref, other_ref, ss_ref, xt_ref):
    half = inv_ref.shape[0]
    full = half * 3 // 2
    upper = is_upper(level)
    _, oo2 = order(upper, own_ref[:half, :], other_ref[:half, :])
    _, os2 = order(upper, own_ref[half : half + full, :], other_ref[half : half + full, :])
    os2 = unpack_full(os2)
    xt2 = mm(os2, inv_ref[...])
    xt_ref[...] = xt2
    ss_ref[...] = oo2 - pack_symmetric(mm_nt(xt2, os2))


def split_rhs(upper, own_f, other_f):
    own, other = to_row(own_f), to_row(other_f)
    first, second = order(upper, own, other)
    half = own.shape[1] // 2
    return own[:, half:] + other[:, half:], jnp.concatenate([first[:, :half], second[:, :half]], axis=1)


def merge(upper, inverse, xt2, os1, os2, own_f, other_f):
    half = inverse.shape[0]
    shared, outer = split_rhs(upper, own_f, other_f)
    xt = mm(jnp.concatenate([os1, jnp.broadcast_to(shared, (8, half))], axis=0), inverse)
    z = xt[half : half + 1]
    both = mm_nt(xt, jnp.concatenate([os1, os2], axis=0))
    cross = -both[:half, half:]
    f = outer - both[half : half + 1]
    return jnp.concatenate([xt[:half], xt2], axis=0), z, both[:half, :half], cross, f


def put_rest(rest_ref, oo, cross, f):
    half = cross.shape[0]
    full = half * 3 // 2
    rest_ref[:half, :] = oo
    rest_ref[half : half + full, :] = pack_full(cross)
    rest_ref[half + full :, :] = from_row(f)


def first_rest_kernel(inv_ref, xt2_ref, own_ref, other_ref, own_f_ref, other_f_ref, rest_ref, xt_ref, z_ref):
    half = inv_ref.shape[0]
    upper = is_upper(0)
    os1, os2 = order(upper, own_ref[:half, half:], other_ref[:half, half:])
    oo1, _ = order(upper, own_ref[:half, :half], other_ref[:half, :half])
    xt_ref[...], z_ref[...], less, cross, f = merge(
        upper, inv_ref[...], xt2_ref[...], os1, os2, own_f_ref[...], other_f_ref[...]
    )
    put_rest(rest_ref, pack_symmetric(oo1 - less), cross, f)


def unpacked(upper, own_ref, other_ref, half):
    full = half * 3 // 2
    oo1, oo2 = order(upper, own_ref[:half, :], other_ref[:half, :])
    os1, os2 = order(upper, own_ref[half : half + full, :], other_ref[half : half + full, :])
    return unpack_full(os1), unpack_full(os2), oo1, oo2, own_ref[half + full :, :], other_ref[half + full :, :]


def rest_kernel(level, inv_ref, xt2_ref, own_ref, other_ref, rest_ref, xt_ref, z_ref):
    upper = is_upper(level)
    os1, os2, oo1, _, own_f, other_f = unpacked(upper, own_ref, other_ref, inv_ref.shape[0])
    xt_ref[...], z_ref[...], less, cross, f = merge(
        upper, inv_ref[...], xt2_ref[...], os1, os2, own_f, other_f
    )
    put_rest(rest_ref, oo1 - pack_symmetric(less), cross, f)


def end_kernel(level, inv_ref, own_ref, other_ref, t_ref, xt_ref, z_ref, yt_ref, w_ref):
    half = inv_ref.shape[0]
    upper = is_upper(level)
    os1, os2, oo1, oo2, own_f, other_f = unpacked(upper, own_ref, other_ref, half)
    xt1 = mm(os1, inv_ref[...])
    less = mm_nt(xt1, os1)
    oo = unpack_symmetric(oo1)
    inverse = invert([rows - less[i * panel : (i + 1) * panel] for i, rows in enumerate(oo)])
    xt2 = mm(os2, inv_ref[...])
    less_shared = mm_nt(xt2, os2)
    shared, outer = split_rhs(upper, own_f, other_f)
    z = mm(shared, inv_ref[...])
    cross = -mm_nt(xt1, os2)
    f = outer - jnp.concatenate([mm_nt(z, os1), mm_nt(z, os2)], axis=1)
    xt_ref[:half, :] = xt1
    xt_ref[half:, :] = xt2
    z_ref[...] = z
    stacked = jnp.concatenate([cross.T, jnp.broadcast_to(f[:, :half], (8, half))], axis=0)
    yt = mm(stacked, inverse)
    w = yt[half : half + 1]
    yt_ref[...] = yt[:half]
    w_ref[...] = w
    t_ref[:half, :] = oo2 - pack_symmetric(less_shared + mm(yt[:half], cross))
    rest = jnp.concatenate([f[:, half:] - mm(w, cross), jnp.zeros((1, half), jnp.float32)], axis=1)
    t_ref[half:, :] = from_row(rest)


def compose_kernel(levels, yt_ref, w_ref, *refs):
    half = yt_ref.shape[0]
    out_ref = refs[-1]
    row = lax.broadcasted_iota(jnp.int32, (half + 8, half), 0)
    col = lax.broadcasted_iota(jnp.int32, (half + 8, half), 1)
    outer = jnp.concatenate([-yt_ref[...], jnp.broadcast_to(w_ref[...], (8, half))], axis=0)
    answer = jnp.concatenate([outer, jnp.where(row == col, 1.0, 0.0)], axis=1)
    for level in reversed(range(levels)):
        inner = jnp.where(row >= half, refs[2 * level + 1][...], 0.0) - mm(answer, refs[2 * level][...])
        outer = jnp.where(is_upper(level), answer[:, half:], answer[:, :half])
        answer = jnp.concatenate([outer, inner], axis=1)
    out_ref[...] = answer


def solve_kernel(own_ref, other_ref, map_ref, out_ref):
    half = map_ref.shape[0] - 8
    width = map_ref.shape[1]
    total = own_ref[...] + other_ref[...]
    right = jnp.broadcast_to(to_row(total[half:])[:, :half], (8, half)).T
    pad = jnp.zeros((panel, lanes - half % lanes - 8), jnp.float32)
    slabs = [
        jnp.concatenate([rows, right[i * panel : (i + 1) * panel], pad], axis=1)
        for i, rows in enumerate(unpack_symmetric(total[:half]))
    ]
    shared = invert(slabs, forget=True)[:, half % lanes : half % lanes + 1]
    parts = jnp.broadcast_to(shared, (half, width)) * map_ref[:half, :]
    out_ref[...] = jnp.sum(parts, axis=0, keepdims=True) + map_ref[half : half + 1, :]


vmem = pl.BlockSpec(memory_space=pltpu.VMEM)


def call(kernel, name, shapes, micros, *operands):
    outs = tuple(jax.ShapeDtypeStruct(s, jnp.float32) for s in shapes)
    single = len(outs) == 1
    return pl.pallas_call(
        kernel,
        out_shape=outs[0] if single else outs,
        in_specs=[vmem] * len(operands),
        out_specs=vmem if single else tuple(vmem for _ in outs),
        compiler_params=pltpu.CompilerParams(vmem_limit_bytes=32 << 20),
        cost_estimate=pl.CostEstimate(flops=int(micros * 1e9), bytes_accessed=0, transcendentals=0),
        name=name,
    )(*operands)


def partner(array, level):
    count = lax.axis_size(everywhere)
    return lax.ppermute(array, everywhere, [(i, i ^ 1 << level) for i in range(count)])


def halos(state):
    chans, rows, cells = state.shape
    axial, azim = lax.axis_size("axial"), lax.axis_size("azim")
    top, bottom, sides = call(
        edges_kernel, "edges", [(chans, cells), (chans, cells), (2 * chans, rows)], 0.5, state
    )
    up = [(i, i + 1) for i in range(axial - 1)]
    before = lax.ppermute(bottom, "axial", up)
    after = lax.ppermute(top, "axial", [(j, i) for i, j in up])
    around = [(i, (i + 1) % azim) for i in range(azim)]
    if azim == 2:
        sides = lax.ppermute(sides, "azim", around)
    else:
        left = lax.ppermute(sides[chans:], "azim", around)
        right = lax.ppermute(sides[:chans], "azim", [(j, i) for i, j in around])
        sides = jnp.concatenate([right, left], axis=0)
    return before, after, sides


def body(adjoint_state, adjoint_source, reaction_rate, jacobian, lifting, separator, leaf_schur):
    chans, rows, cells = adjoint_state.shape[1:]
    width = leaf_schur.shape[-1]
    half = width // 2
    full = half * 3 // 2
    levels = lax.axis_size(everywhere).bit_length() - 1
    rest_shapes = [(half + full + 8, lanes), (width, half), (1, half)]

    schur = leaf_schur.reshape(width, width)
    other_schur = partner(schur, 0)
    state = adjoint_state.reshape(chans, rows, cells)
    edges = halos(state)
    ss, inverse, xt2 = call(
        first_kernel, "factor_0", [(half, lanes), (half, half), (half, half)], 8.0, schur, other_schur
    )
    other_ss = partner(ss, 1)
    f = call(
        leaf_kernel,
        "leaf_rhs",
        [(8, lanes)],
        2.3,
        separator.reshape(1, -1),
        ss,
        state,
        adjoint_source.reshape(chans, rows, cells),
        reaction_rate.reshape(rows, cells),
        jacobian.reshape(chans, chans),
        lifting.reshape(-1, rows, cells),
        *edges,
    )
    rest, xt, z = call(
        first_rest_kernel, "rest_0", rest_shapes, 0.05, inverse, xt2, schur, other_schur, f, partner(f, 0)
    )
    other_rest = partner(rest, 1)
    saved = [xt, z]
    for level in range(1, levels - 1):
        inverse = call(factor_kernel, f"factor_{level}", [(half, half)], 6.5, ss, other_ss)
        if level < levels - 2:
            ss, xt2 = call(
                functools.partial(shared_kernel, level),
                f"shared_{level}",
                [(half, lanes), (half, half)],
                1.5,
                inverse,
                rest,
                other_rest,
            )
            other_ss = partner(ss, level + 1)
            rest, xt, z = call(
                functools.partial(rest_kernel, level), f"rest_{level}", rest_shapes, 0.05, inverse, xt2, rest, other_rest
            )
            other_rest = partner(rest, level + 1)
        else:
            end, xt, z, yt, w = call(
                functools.partial(end_kernel, level),
                f"end_{level}",
                [(half + 8, lanes), (width, half), (1, half), (half, half), (1, half)],
                9.5,
                inverse,
                rest,
                other_rest,
            )
        saved += [xt, z]
    other_end = partner(end, levels - 1)
    composed = call(
        functools.partial(compose_kernel, levels - 1), "compose", [(half + 8, width)], 3.7, yt, w, *saved
    )
    answer = call(solve_kernel, "solve", [(1, width)], 7.0, end, other_end, composed)
    return answer.reshape(1, 1, 1, width)


def solution(mesh):
    in_specs = (
        P("bank", None, "axial", "azim"),
        P("bank", None, "axial", "azim"),
        P("bank", "axial", "azim"),
        P("bank", None, None),
        P("bank", None, "axial", "azim"),
        P("axial", "azim", "bank", None),
        P("axial", "azim", "bank", None, None),
    )
    out_specs = P("axial", "azim", "bank", None)
    return jax.shard_map(body, mesh=mesh, in_specs=in_specs, out_specs=out_specs, check_vma=False)
```

profile of v0, /device:TPU:0, one launch (start us, length us, event | category | flops | bytes accessed | tf_op | source)
XLA Modules:
  0.0 73.3 jit_solution(1476728957115360196)
XLA Ops:
  0.0 0.5 collective-permute-start
  0.5 0.0 copy-start.1
  0.5 1.0 %copy-done.1 = f32[1,64,8,256]{3,2,1,0:T(8,128)S(1)} copy-done((f32[1,64,8,256]{3,2,1,0:T(8,128)S(1)}, f32[1,64,8,256]{3,2,1,0:T(8,128)}, u32[]{:S(2)}) %copy-start.1) | copy-done | bytes 524312
  1.5 0.0 copy-start
  1.5 0.3 edges.1
  1.8 4.4 %collective-permute-start.2 = (f32[64,256]{1,0:T(8,128)S(1)}, f32[64,256]{1,0:T(8,128)S(1)}, u32[]{:S(2)}, u32[]{:S(2)}) collective-permute-start(f32[64,256]{1,0:T(8,128)S(1)} %get-tuple-element.32), channel_id=1, source_target_pairs={{0,4},{4,8},{8,12},{12,16},{16,20},{20,24},{24,28},{1,5},{5,9},{9,... | collective-permute-start | bytes 196616 | tf_op jit(solution)/shard_map/ppermute | solution.py:391
  6.2 1.3 %collective-permute-start.3 = (f32[64,256]{1,0:T(8,128)S(1)}, f32[64,256]{1,0:T(8,128)S(1)}, u32[]{:S(2)}, u32[]{:S(2)}) collective-permute-start(f32[64,256]{1,0:T(8,128)S(1)} %get-tuple-element.33), channel_id=1, source_target_pairs={{4,0},{8,4},{12,8},{16,12},{20,16},{24,20},{28,24},{5,1},{9,5},{13... | collective-permute-start | bytes 196616 | tf_op jit(solution)/shard_map/ppermute | solution.py:392
  7.5 0.0 copy-start.2
  7.5 0.0 copy-start.3
  7.5 0.0 copy-start.4
  7.5 0.0 copy-start.5
  7.5 1.6 %collective-permute-start.4 = (f32[128,8]{1,0:T(8,128)S(1)}, f32[128,8]{1,0:T(8,128)S(1)}, u32[]{:S(2)}, u32[]{:S(2)}) collective-permute-start(f32[128,8]{1,0:T(8,128)S(1)} %get-tuple-element.34), channel_id=1, source_target_pairs={{0,2},{2,0},{1,3},{3,1},{4,6},{6,4},{5,7},{7,5},{8,10},{10,8},{9,1... | collective-permute-start | bytes 12296 | tf_op jit(solution)/shard_map/ppermute | solution.py:395
  9.1 0.0 collective-permute-done.other_ref
  9.1 0.0 copy-done
  9.1 6.4 %factor_0.1 = (f32[192,128]{1,0:T(8,128)S(1)}, f32[192,192]{1,0:T(8,128)S(1)}, f32[192,192]{1,0:T(8,128)S(1)}) custom-call(f32[384,384]{1,0:T(8,128)S(1)} %bitcast.9, f32[384,384]{1,0:T(8,128)S(1)} %collective-permute-done.other_ref), custom_call_target="tpu_custom_call" | custom-call | flops 8000000000 | tf_op jit(solution)/shard_map/factor_0/pallas_call | solution.py:368
  15.5 0.0 copy-start.6
  15.5 0.6 collective-permute-start.1
  16.1 0.0 collective-permute-done.4.sides_ref
  16.1 0.0 collective-permute-done.2.before_ref
  16.1 0.0 collective-permute-done.3.after_ref
  16.1 0.0 copy-start.7
  16.1 0.0 copy-done.2
  16.1 0.0 copy-done.3
  16.1 0.0 copy-done.4
  16.1 0.0 copy-done.5
  16.1 0.1 copy-done.6
  16.2 0.6 copy-done.7
  16.8 1.0 %leaf_rhs.1.own_f_ref = f32[8,128]{1,0:T(8,128)S(1)} custom-call(s32[1,6]{1,0:T(1,128)S(1)} %bitcast.17, f32[192,128]{1,0:T(8,128)S(1)} %get-tuple-element.29.own_ref.after_this_ref, f32[64,8,256]{2,1,0:T(8,128)S(1)} %bitcast.12, f32[64,8,256]{2,1,0:T(8,128)S(1)} %bitcast.13, f32[8,256]{1,0:T(8,128)S(1)} %bitcast.16, f32[64,64]{1,0:T(8,128)S(1)} %bitcast.15, ...), custom_call_target="tpu_custom_call" | custom-call | flops 2300000000 | tf_op jit(solution)/shard_map/leaf_rhs/pallas_call | solution.py:368
  17.7 0.0 collective-permute-start.5
  17.7 1.2 %collective-permute-done.5.other_f_ref = f32[8,128]{1,0:T(8,128)S(1)} collective-permute-done((f32[8,128]{1,0:T(8,128)S(1)}, f32[8,128]{1,0:T(8,128)S(1)}, u32[]{:S(2)}, u32[]{:S(2)}) %collective-permute-start.5) | collective-permute-done | bytes 4128 | tf_op jit(solution)/shard_map/ppermute | solution.py:381
  18.9 1.1 %rest_0.1 = (f32[488,128]{1,0:T(8,128)S(1)}, f32[384,192]{1,0:T(8,128)S(1)}, f32[1,192]{1,0:T(1,128)S(1)}) custom-call(f32[192,192]{1,0:T(8,128)S(1)} %get-tuple-element.30.inv_ref, f32[192,192]{1,0:T(8,128)S(1)} %get-tuple-element.31.xt2_ref, f32[384,384]{1,0:T(8,128)S(1)} %bitcast.10, f32[384,384]{1,0:T(8,128)S(1)} %collective-permute-done.other_ref, ...), custom_call_target="tpu_custom_call" | custom-call | flops 50000000 | tf_op jit(solution)/shard_map/rest_0/pallas_call | solution.py:368
  20.0 1.6 %collective-permute-start.6 = (f32[488,128]{1,0:T(8,128)S(1)}, f32[488,128]{1,0:T(8,128)S(1)}, u32[]{:S(2)}, u32[]{:S(2)}) collective-permute-start(f32[488,128]{1,0:T(8,128)S(1)} %get-tuple-element.35.own_ref), channel_id=1, source_target_pairs={{0,2},{1,3},{2,0},{3,1},{4,6},{5,7},{6,4},{7,5},{8,10},{9,11},{10,... | collective-permute-start | bytes 749576 | tf_op jit(solution)/shard_map/ppermute | solution.py:381
  21.5 0.0 collective-permute-done.1.other_ref
  21.5 4.9 %factor_1.1.inv_ref = f32[192,192]{1,0:T(8,128)S(1)} custom-call(f32[192,128]{1,0:T(8,128)S(1)} %get-tuple-element.29.own_ref.after_this_ref, f32[192,128]{1,0:T(8,128)S(1)} %collective-permute-done.1.other_ref), custom_call_target="tpu_custom_call" | custom-call | flops 6499999744 | tf_op jit(solution)/shard_map/factor_1/pallas_call | solution.py:368
  26.5 1.7 %collective-permute-done.6.other_ref = f32[488,128]{1,0:T(8,128)S(1)} collective-permute-done((f32[488,128]{1,0:T(8,128)S(1)}, f32[488,128]{1,0:T(8,128)S(1)}, u32[]{:S(2)}, u32[]{:S(2)}) %collective-permute-start.6) | collective-permute-done | bytes 249888 | tf_op jit(solution)/shard_map/ppermute | solution.py:381
  28.1 0.9 %shared_1.1 = (f32[192,128]{1,0:T(8,128)S(1)}, f32[192,192]{1,0:T(8,128)S(1)}) custom-call(f32[192,192]{1,0:T(8,128)S(1)} %factor_1.1.inv_ref, f32[488,128]{1,0:T(8,128)S(1)} %get-tuple-element.35.own_ref, f32[488,128]{1,0:T(8,128)S(1)} %collective-permute-done.6.other_ref), custom_call_target="tpu_custom_call" | custom-call | flops 1500000000 | tf_op jit(solution)/shard_map/shared_1/pallas_call | solution.py:368
  29.0 2.7 %collective-permute-start.7 = (f32[192,128]{1,0:T(8,128)S(1)}, f32[192,128]{1,0:T(8,128)S(1)}, u32[]{:S(2)}, u32[]{:S(2)}) collective-permute-start(f32[192,128]{1,0:T(8,128)S(1)} %get-tuple-element.36.own_ref), channel_id=1, source_target_pairs={{0,4},{1,5},{2,6},{3,7},{4,0},{5,1},{6,2},{7,3},{8,12},{9,13},{10,... | collective-permute-start | bytes 294920 | tf_op jit(solution)/shard_map/ppermute | solution.py:381
  31.7 1.2 %rest_1.1 = (f32[488,128]{1,0:T(8,128)S(1)}, f32[384,192]{1,0:T(8,128)S(1)}, f32[1,192]{1,0:T(1,128)S(1)}) custom-call(f32[192,192]{1,0:T(8,128)S(1)} %factor_1.1.inv_ref, f32[192,192]{1,0:T(8,128)S(1)} %get-tuple-element.37.xt2_ref, f32[488,128]{1,0:T(8,128)S(1)} %get-tuple-element.35.own_ref, f32[488,128]{1,0:T(8,128)S(1)} %collective-permute-done.6.other_ref), custom_call_target="tpu_custom_call" | custom-call | flops 50000000 | tf_op jit(solution)/shard_map/rest_1/pallas_call | solution.py:368
  33.0 0.1 collective-permute-start.8
  33.0 1.9 %collective-permute-done.7.other_ref = f32[192,128]{1,0:T(8,128)S(1)} collective-permute-done((f32[192,128]{1,0:T(8,128)S(1)}, f32[192,128]{1,0:T(8,128)S(1)}, u32[]{:S(2)}, u32[]{:S(2)}) %collective-permute-start.7) | collective-permute-done | bytes 98336 | tf_op jit(solution)/shard_map/ppermute | solution.py:381
  34.9 4.9 %factor_2.1.inv_ref = f32[192,192]{1,0:T(8,128)S(1)} custom-call(f32[192,128]{1,0:T(8,128)S(1)} %get-tuple-element.36.own_ref, f32[192,128]{1,0:T(8,128)S(1)} %collective-permute-done.7.other_ref), custom_call_target="tpu_custom_call" | custom-call | flops 6499999744 | tf_op jit(solution)/shard_map/factor_2/pallas_call | solution.py:368
  39.9 0.2 collective-permute-done.8.other_ref
  40.0 0.9 %shared_2.1 = (f32[192,128]{1,0:T(8,128)S(1)}, f32[192,192]{1,0:T(8,128)S(1)}) custom-call(f32[192,192]{1,0:T(8,128)S(1)} %factor_2.1.inv_ref, f32[488,128]{1,0:T(8,128)S(1)} %get-tuple-element.38.own_ref, f32[488,128]{1,0:T(8,128)S(1)} %collective-permute-done.8.other_ref), custom_call_target="tpu_custom_call" | custom-call | flops 1500000000 | tf_op jit(solution)/shard_map/shared_2/pallas_call | solution.py:368
  41.0 3.4 %collective-permute-start.9 = (f32[192,128]{1,0:T(8,128)S(1)}, f32[192,128]{1,0:T(8,128)S(1)}, u32[]{:S(2)}, u32[]{:S(2)}) collective-permute-start(f32[192,128]{1,0:T(8,128)S(1)} %get-tuple-element.39.own_ref), channel_id=1, source_target_pairs={{0,8},{1,9},{2,10},{3,11},{4,12},{5,13},{6,14},{7,15},{8,0},{9,1},... | collective-permute-start | bytes 294920 | tf_op jit(solution)/shard_map/ppermute | solution.py:381
  44.3 1.1 %rest_2.1 = (f32[488,128]{1,0:T(8,128)S(1)}, f32[384,192]{1,0:T(8,128)S(1)}, f32[1,192]{1,0:T(1,128)S(1)}) custom-call(f32[192,192]{1,0:T(8,128)S(1)} %factor_2.1.inv_ref, f32[192,192]{1,0:T(8,128)S(1)} %get-tuple-element.40.xt2_ref, f32[488,128]{1,0:T(8,128)S(1)} %get-tuple-element.38.own_ref, f32[488,128]{1,0:T(8,128)S(1)} %collective-permute-done.8.other_ref), custom_call_target="tpu_custom_call" | custom-call | flops 50000000 | tf_op jit(solution)/shard_map/rest_2/pallas_call | solution.py:368
  45.4 0.1 collective-permute-start.10
  45.4 2.3 %collective-permute-done.9.other_ref = f32[192,128]{1,0:T(8,128)S(1)} collective-permute-done((f32[192,128]{1,0:T(8,128)S(1)}, f32[192,128]{1,0:T(8,128)S(1)}, u32[]{:S(2)}, u32[]{:S(2)}) %collective-permute-start.9) | collective-permute-done | bytes 98336 | tf_op jit(solution)/shard_map/ppermute | solution.py:381
  47.8 4.9 %factor_3.1.inv_ref = f32[192,192]{1,0:T(8,128)S(1)} custom-call(f32[192,128]{1,0:T(8,128)S(1)} %get-tuple-element.39.own_ref, f32[192,128]{1,0:T(8,128)S(1)} %collective-permute-done.9.other_ref), custom_call_target="tpu_custom_call" | custom-call | flops 6499999744 | tf_op jit(solution)/shard_map/factor_3/pallas_call | solution.py:368
  52.7 0.0 collective-permute-done.10.other_ref
  52.7 8.4 %end_3.1 = (f32[200,128]{1,0:T(8,128)S(1)}, f32[384,192]{1,0:T(8,128)S(1)}, f32[1,192]{1,0:T(1,128)S(1)}, f32[192,192]{1,0:T(8,128)S(1)}, f32[1,192]{1,0:T(1,128)S(1)}) custom-call(f32[192,192]{1,0:T(8,128)S(1)} %factor_3.1.inv_ref, f32[488,128]{1,0:T(8,128)S(1)} %get-tuple-element.41.own_ref, f32[488,128]{1,0:T(8,128)S(1)} %collective-permute-done.10.other_ref), custom_call_target="tpu_custom_call" | custom-call | flops 9500000256 | tf_op jit(solution)/shard_map/end_3/pallas_call | solution.py:368
  61.2 3.3 %collective-permute-start.11 = (f32[200,128]{1,0:T(8,128)S(1)}, f32[200,128]{1,0:T(8,128)S(1)}, u32[]{:S(2)}, u32[]{:S(2)}) collective-permute-start(f32[200,128]{1,0:T(8,128)S(1)} %get-tuple-element.42.own_ref), channel_id=1, source_target_pairs={{0,16},{1,17},{2,18},{3,19},{4,20},{5,21},{6,22},{7,23},{8,24},{9,... | collective-permute-start | bytes 307208 | tf_op jit(solution)/shard_map/ppermute | solution.py:381
  64.5 3.2 %compose.1.map_ref = f32[200,384]{1,0:T(8,128)S(1)} custom-call(f32[192,192]{1,0:T(8,128)S(1)} %get-tuple-element.43.yt_ref, f32[1,192]{1,0:T(1,128)S(1)} %get-tuple-element.44.w_ref, f32[384,192]{1,0:T(8,128)S(1)} %get-tuple-element.45.refs_0_, f32[1,192]{1,0:T(1,128)S(1)} %get-tuple-element.46.refs_1_, f32[384,192]{1,0:T(8,128)S(1)} %get-tuple-element.47.refs_2_, ...), custom_call_target="tpu_custom_call" | custom-call | flops 3700000000 | tf_op jit(solution)/shard_map/compose/pallas_call | solution.py:368
  67.7 0.0 collective-permute-done.11.other_ref
  67.7 5.6 %solve.1 = f32[1,384]{1,0:T(1,128)} custom-call(f32[200,128]{1,0:T(8,128)S(1)} %get-tuple-element.42.own_ref, f32[200,128]{1,0:T(8,128)S(1)} %collective-permute-done.11.other_ref, f32[200,384]{1,0:T(8,128)S(1)} %compose.1.map_ref), custom_call_target="tpu_custom_call" | custom-call | flops 7000000000 | tf_op jit(solution)/shard_map/solve/pallas_call | solution.py:368
Async XLA Ops:
  0.0 9.1 %collective-permute-start = (f32[384,384]{1,0:T(8,128)}, f32[384,384]{1,0:T(8,128)S(1)}, u32[]{:S(2)}, u32[]{:S(2)}) collective-permute-start(f32[384,384]{1,0:T(8,128)} %bitcast.8), channel_id=1, source_target_pairs={{0,1},{1,0},{2,3},{3,2},{4,5},{5,4},{6,7},{7,6},{8,9},{9,8},{10,11... | collective-permute-start | bytes 1769480 | tf_op jit(solution)/shard_map/ppermute | solution.py:381
  0.5 1.0 %copy-start.1 = (f32[1,64,8,256]{3,2,1,0:T(8,128)S(1)}, f32[1,64,8,256]{3,2,1,0:T(8,128)}, u32[]{:S(2)}) copy-start(f32[1,64,8,256]{3,2,1,0:T(8,128)} %param.7) | copy-start | bytes 1572868
  1.5 7.6 %copy-start = (f32[1,1,1,384,384]{4,3,2,1,0:T(8,128)S(1)}, f32[1,1,1,384,384]{4,3,2,1,0:T(8,128)}, u32[]{:S(2)}) copy-start(f32[1,1,1,384,384]{4,3,2,1,0:T(8,128)} %param.13) | copy-start | bytes 1769476
  1.8 14.3 %collective-permute-start.2 = (f32[64,256]{1,0:T(8,128)S(1)}, f32[64,256]{1,0:T(8,128)S(1)}, u32[]{:S(2)}, u32[]{:S(2)}) collective-permute-start(f32[64,256]{1,0:T(8,128)S(1)} %get-tuple-element.32), channel_id=1, source_target_pairs={{0,4},{4,8},{8,12},{12,16},{16,20},{20,24},{24,28},{1,5},{5,9},{9,... | collective-permute-start | bytes 196616 | tf_op jit(solution)/shard_map/ppermute | solution.py:391
  6.2 9.9 %collective-permute-start.3 = (f32[64,256]{1,0:T(8,128)S(1)}, f32[64,256]{1,0:T(8,128)S(1)}, u32[]{:S(2)}, u32[]{:S(2)}) collective-permute-start(f32[64,256]{1,0:T(8,128)S(1)} %get-tuple-element.33), channel_id=1, source_target_pairs={{4,0},{8,4},{12,8},{16,12},{20,16},{24,20},{28,24},{5,1},{9,5},{13... | collective-permute-start | bytes 196616 | tf_op jit(solution)/shard_map/ppermute | solution.py:392
  7.5 8.6 %copy-start.2 = (f32[1,64,8,256]{3,2,1,0:T(8,128)S(1)}, f32[1,64,8,256]{3,2,1,0:T(8,128)}, u32[]{:S(2)}) copy-start(f32[1,64,8,256]{3,2,1,0:T(8,128)} %param.7) | copy-start | bytes 1572868
  7.5 8.6 %copy-start.3 = (f32[1,64,8,256]{3,2,1,0:T(8,128)S(1)}, f32[1,64,8,256]{3,2,1,0:T(8,128)}, u32[]{:S(2)}) copy-start(f32[1,64,8,256]{3,2,1,0:T(8,128)} %param.8) | copy-start | bytes 1572868
  7.5 8.6 %copy-start.4 = (f32[1,6,8,256]{3,2,1,0:T(8,128)S(1)}, f32[1,6,8,256]{3,2,1,0:T(8,128)}, u32[]{:S(2)}) copy-start(f32[1,6,8,256]{3,2,1,0:T(8,128)} %param.11) | copy-start | bytes 147460
  7.5 8.6 %copy-start.5 = (f32[1,64,64]{2,1,0:T(8,128)S(1)}, f32[1,64,64]{2,1,0:T(8,128)}, u32[]{:S(2)}) copy-start(f32[1,64,64]{2,1,0:T(8,128)} %param.10) | copy-start | bytes 49156
  7.5 8.6 %collective-permute-start.4 = (f32[128,8]{1,0:T(8,128)S(1)}, f32[128,8]{1,0:T(8,128)S(1)}, u32[]{:S(2)}, u32[]{:S(2)}) collective-permute-start(f32[128,8]{1,0:T(8,128)S(1)} %get-tuple-element.34), channel_id=1, source_target_pairs={{0,2},{2,0},{1,3},{3,1},{4,6},{6,4},{5,7},{7,5},{8,10},{10,8},{9,1... | collective-permute-start | bytes 12296 | tf_op jit(solution)/shard_map/ppermute | solution.py:395
  15.5 0.7 copy-start.6
  15.5 6.0 %collective-permute-start.1 = (f32[192,128]{1,0:T(8,128)S(1)}, f32[192,128]{1,0:T(8,128)S(1)}, u32[]{:S(2)}, u32[]{:S(2)}) collective-permute-start(f32[192,128]{1,0:T(8,128)S(1)} %get-tuple-element.29.own_ref.after_this_ref), channel_id=1, source_target_pairs={{0,2},{1,3},{2,0},{3,1},{4,6},{5,7},{6,4},{7,5},{8,10},{9,11},{10,... | collective-permute-start | bytes 294920 | tf_op jit(solution)/shard_map/ppermute | solution.py:381
  16.1 0.7 copy-start.7
  17.7 1.2 %collective-permute-start.5 = (f32[8,128]{1,0:T(8,128)S(1)}, f32[8,128]{1,0:T(8,128)S(1)}, u32[]{:S(2)}, u32[]{:S(2)}) collective-permute-start(f32[8,128]{1,0:T(8,128)S(1)} %leaf_rhs.1.own_f_ref), channel_id=1, source_target_pairs={{0,1},{1,0},{2,3},{3,2},{4,5},{5,4},{6,7},{7,6},{8,9},{9,8},{10,11... | collective-permute-start | bytes 12296 | tf_op jit(solution)/shard_map/ppermute | solution.py:381
  20.0 8.2 %collective-permute-start.6 = (f32[488,128]{1,0:T(8,128)S(1)}, f32[488,128]{1,0:T(8,128)S(1)}, u32[]{:S(2)}, u32[]{:S(2)}) collective-permute-start(f32[488,128]{1,0:T(8,128)S(1)} %get-tuple-element.35.own_ref), channel_id=1, source_target_pairs={{0,2},{1,3},{2,0},{3,1},{4,6},{5,7},{6,4},{7,5},{8,10},{9,11},{10,... | collective-permute-start | bytes 749576 | tf_op jit(solution)/shard_map/ppermute | solution.py:381
  29.0 5.9 %collective-permute-start.7 = (f32[192,128]{1,0:T(8,128)S(1)}, f32[192,128]{1,0:T(8,128)S(1)}, u32[]{:S(2)}, u32[]{:S(2)}) collective-permute-start(f32[192,128]{1,0:T(8,128)S(1)} %get-tuple-element.36.own_ref), channel_id=1, source_target_pairs={{0,4},{1,5},{2,6},{3,7},{4,0},{5,1},{6,2},{7,3},{8,12},{9,13},{10,... | collective-permute-start | bytes 294920 | tf_op jit(solution)/shard_map/ppermute | solution.py:381
  33.0 7.0 %collective-permute-start.8 = (f32[488,128]{1,0:T(8,128)S(1)}, f32[488,128]{1,0:T(8,128)S(1)}, u32[]{:S(2)}, u32[]{:S(2)}) collective-permute-start(f32[488,128]{1,0:T(8,128)S(1)} %get-tuple-element.38.own_ref), channel_id=1, source_target_pairs={{0,4},{1,5},{2,6},{3,7},{4,0},{5,1},{6,2},{7,3},{8,12},{9,13},{10,... | collective-permute-start | bytes 749576 | tf_op jit(solution)/shard_map/ppermute | solution.py:381
  41.0 6.8 %collective-permute-start.9 = (f32[192,128]{1,0:T(8,128)S(1)}, f32[192,128]{1,0:T(8,128)S(1)}, u32[]{:S(2)}, u32[]{:S(2)}) collective-permute-start(f32[192,128]{1,0:T(8,128)S(1)} %get-tuple-element.39.own_ref), channel_id=1, source_target_pairs={{0,8},{1,9},{2,10},{3,11},{4,12},{5,13},{6,14},{7,15},{8,0},{9,1},... | collective-permute-start | bytes 294920 | tf_op jit(solution)/shard_map/ppermute | solution.py:381
  45.4 7.3 %collective-permute-start.10 = (f32[488,128]{1,0:T(8,128)S(1)}, f32[488,128]{1,0:T(8,128)S(1)}, u32[]{:S(2)}, u32[]{:S(2)}) collective-permute-start(f32[488,128]{1,0:T(8,128)S(1)} %get-tuple-element.41.own_ref), channel_id=1, source_target_pairs={{0,8},{1,9},{2,10},{3,11},{4,12},{5,13},{6,14},{7,15},{8,0},{9,1},... | collective-permute-start | bytes 749576 | tf_op jit(solution)/shard_map/ppermute | solution.py:381
  61.2 6.5 %collective-permute-start.11 = (f32[200,128]{1,0:T(8,128)S(1)}, f32[200,128]{1,0:T(8,128)S(1)}, u32[]{:S(2)}, u32[]{:S(2)}) collective-permute-start(f32[200,128]{1,0:T(8,128)S(1)} %get-tuple-element.42.own_ref), channel_id=1, source_target_pairs={{0,16},{1,17},{2,18},{3,19},{4,20},{5,21},{6,22},{7,23},{8,24},{9,... | collective-permute-start | bytes 307208 | tf_op jit(solution)/shard_map/ppermute | solution.py:381
where the time goes:
time: 73.5 us; the launch traced here: 73.3 us
  Pallas kernels  44.8 us (61%)
  starting transfers between devices  19.4 us (26%)
  waiting for transfers between devices  7.24 us (10%)
  local copies, waits for them, and re-layouts  1.68 us (2%)
    pallas_call x14, Pallas kernels, call(): pl.pallas_call(kernel, out_shape=outs[0] if single else outs, in_specs=[v...  44.8 us
    ppermute x9, starting transfers between devices, partner(): lax.ppermute(array, everywhere, [(i, i ^ 1 << level) for i in range(count)])  12.1 us
    ppermute x9, waiting for transfers between devices, partner(): lax.ppermute(array, everywhere, [(i, i ^ 1 << level) for i in range(count)])  7.23 us
    ppermute x1, starting transfers between devices, halos(): before = lax.ppermute(bottom, 'axial', up)  4.4 us
    unnamed x16, local copies, waits for them, and re-layouts  1.68 us
    ppermute x1, starting transfers between devices, halos(): sides = lax.ppermute(sides, 'azim', around)  1.58 us
  transfers between devices with their start and end apart: 12, of which 5 were waited for; matrix products, arithmetic and copies ran while one was open for 0% of the time, Pallas kernels for 39%

commit v1 on v0

v1 whole, which is shorter than its diff:
```python
import functools

import jax
import jax.numpy as jnp
from jax import lax
from jax.experimental import pallas as pl
from jax.experimental.pallas import tpu as pltpu
from jax.sharding import PartitionSpec as P

highest = lax.Precision.HIGHEST
high = lax.Precision.HIGH
everywhere = ("axial", "azim", "bank")
lanes = 128


def mm(a, b, precision=highest):
    return jnp.dot(a, b, precision=precision, preferred_element_type=jnp.float32)


def mm_nt(a, b, precision=highest):
    dims = (((1,), (1,)), ((), ()))
    return lax.dot_general(a, b, dims, precision=precision, preferred_element_type=jnp.float32)


def mm_tn(a, b, precision=highest):
    dims = (((0,), (0,)), ((), ()))
    return lax.dot_general(a, b, dims, precision=precision, preferred_element_type=jnp.float32)


def sweep_panel(groups, first, jobs):
    n = len(groups)
    groups = [list(g) for g in groups]
    widths = [t.shape[1] for t in groups[0]]
    row = lax.broadcasted_iota(jnp.int32, (8, lanes), 0)
    lane_of = [lax.broadcasted_iota(jnp.int32, (8, w), 1) for w in widths]
    row_of = [lax.broadcasted_iota(jnp.int32, (8, w), 0) for w in widths]

    def columns(q, s):
        tile, lane = divmod(first + 8 * s, lanes)
        return [jnp.broadcast_to(groups[q][tile][:, lane + m : lane + m + 1], (8, lanes)) for m in range(8)]

    def across(column, tile):
        return column if widths[tile] == lanes else column[:, : widths[tile]]

    def spread(value, i):
        return jnp.broadcast_to(value[i : i + 1], value.shape)

    def inside(s):
        tile, lane = divmod(first + 8 * s, lanes)
        return tile, lane, (lane_of[tile] >= lane) & (lane_of[tile] < lane + 8)

    def update(q, s, cols, solved):
        home, _, here = inside(s)
        new = []
        for k, tile in enumerate(groups[q]):
            value = jnp.where(here, 0.0, tile) if k == home else tile
            for m in range(8):
                value = value - across(cols[m], k) * spread(solved[k], m)
            new.append(value)
        groups[q] = new

    diag = columns(0, 0)
    cols = {q: columns(q, 0) for q in range(1, n)}
    pending, before, after = [], [], []
    for s in range(n):
        more = s + 1 < n
        if more:
            low, ahead = list(cols[s + 1]), columns(s + 1, s + 1)
        home, lane, here = inside(s)
        own = list(groups[s])
        own[home] = jnp.where(here, jnp.where(lane_of[home] - lane == row_of[home], 1.0, 0.0), own[home])
        before.append(list(own))
        scale = None
        for p in range(8):
            inverse = 1.0 / spread(diag[p], p)
            scale = inverse if scale is None else jnp.where(row == p, inverse, scale)
            factor = jnp.where(row == p, 0.0, diag[p] * inverse)
            if more:
                low_factor = low[p] * inverse
            for j in range(p + 1, 8):
                entry = spread(diag[j], p)
                diag[j] = diag[j] - factor * entry
                if more:
                    low[j] = low[j] - low_factor * entry
            if more:
                for j in range(8):
                    ahead[j] = ahead[j] - low_factor * spread(low[p], j)
            for k in range(len(own)):
                own[k] = own[k] - across(factor, k) * spread(own[k], p)
            for _ in range(-(-len(pending) // (8 - p))):
                q, *rest = pending.pop(0)
                update(q, *rest)
                cols[q] = columns(q, s)
        solved = [tile * across(scale, k) for k, tile in enumerate(own)]
        after.append(solved)
        for q in range(s + 1, n):
            if q < s + 3:
                update(q, s, cols[q], solved)
            else:
                pending.append((q, s, cols[q], solved))
        if more:
            diag = ahead
            if s + 2 < n:
                cols[s + 2] = columns(s + 2, s + 1)
        if jobs:
            jobs.pop(0)()

    def whole(parts):
        return jnp.concatenate([jnp.concatenate(g, axis=1) for g in parts], axis=0)

    return whole(before), whole(after)


def factorize(a, panel, jobs=()):
    n, m = a.shape
    jobs = list(jobs)
    slabs = [a[i : i + panel] for i in range(0, n, panel)]
    lower, scaled = [], []
    for p in range(len(slabs)):
        lo = p * panel
        w = slabs[p]
        groups = [[w[i : i + 8, t : min(t + lanes, m)] for t in range(0, m, lanes)] for i in range(0, panel, 8)]
        g, r = sweep_panel(groups, lo, jobs)
        lane = lax.broadcasted_iota(jnp.int32, (panel, m), 1)
        row = lax.broadcasted_iota(jnp.int32, (panel, m), 0)
        here = (lane >= lo) & (lane < lo + panel)
        ahead = lane >= lo + row // 8 * 8 + 8
        inner = jnp.where(here & ahead, 0.0, r)
        for q in range(p + 1, len(slabs)):
            slabs[q] = jnp.where(here, 0.0, slabs[q]) - mm_tn(g[:, q * panel : (q + 1) * panel], inner)
        drop = ahead & (lane < n)
        lower.append(jnp.where(drop, 0.0, g))
        scaled.append(jnp.where(drop, 0.0, r))
    for job in jobs:
        job()
    return jnp.concatenate(lower, axis=0), jnp.concatenate(scaled, axis=0)


def pack_symmetric(m):
    third = m.shape[0] // 3
    low = jnp.concatenate([m[:third, 2 * third :], m[2 * third :, 2 * third :]], axis=1)
    return jnp.concatenate([m[:third, : 2 * third], m[third : 2 * third, third:], low], axis=0)


def unpack_symmetric(p):
    third = p.shape[0] // 3
    top, mid, low = p[:third], p[third : 2 * third], p[2 * third :]
    rows = [
        jnp.concatenate([top, low[:, :third]], axis=1),
        jnp.concatenate([top[:, third:].T, mid], axis=1),
        jnp.concatenate([low[:, :third].T, mid[:, third:].T, low[:, third:]], axis=1),
    ]
    return jnp.concatenate(rows, axis=0)


def pack_full(m):
    half = m.shape[0] // 2
    tail = jnp.concatenate([m[:half, lanes:], m[half:, lanes:]], axis=1)
    return jnp.concatenate([m[:, :lanes], tail], axis=0)


def unpack_full(p):
    n = p.shape[0] * 2 // 3
    tail = p[n:]
    rest = jnp.concatenate([tail[:, : lanes // 2], tail[:, lanes // 2 :]], axis=0)
    return jnp.concatenate([p[:n], rest], axis=1)


def to_row(f):
    return jnp.concatenate([f[i : i + 1] for i in range(3)], axis=1)


def from_row(row):
    parts = [row[:, i * lanes : (i + 1) * lanes] for i in range(3)]
    return jnp.concatenate(parts + [jnp.zeros((5, lanes), jnp.float32)], axis=0)


def leaf_kernel(where_ref, after_this_ref, state_ref, source_ref, rate_ref, jac_ref, lift_ref, before_ref, after_ref, sides_ref, f_ref):
    seps = lift_ref.shape[0]
    rows = rate_ref.shape[0]
    width = rate_ref.shape[1]
    chans = jac_ref.shape[0]
    lane = lax.broadcasted_iota(jnp.int32, (8, width), 1)
    where = where_ref[:, :1].astype(jnp.int32)
    lift = []
    for i in range(rows):
        own = lift_ref[:, i, :]
        own = jnp.concatenate([own, jnp.zeros((8 - seps, width), jnp.float32)], axis=0)
        lift.append(own + jnp.where(where == lane + i * width, 1.0, 0.0))
    zero = jnp.zeros((8, width), jnp.float32)
    mixed = []
    for i in range(rows):
        own = lift[i]
        around = (lift[i - 1] if i > 0 else zero) + (lift[i + 1] if i + 1 < rows else zero)
        around = around + jnp.where(lane == 0, 0.0, pltpu.roll(own, 1, 1))
        around = around + jnp.where(lane == width - 1, 0.0, pltpu.roll(own, width - 1, 1))
        mixed.append(jnp.concatenate([0.5 * around - 2.0 * own, own * rate_ref[i : i + 1, :]], axis=0))
    state = jnp.concatenate([state_ref[:, i, :] for i in range(rows)], axis=1)
    source = jnp.concatenate([source_ref[:, i, :] for i in range(rows)], axis=1)
    prod = mm_nt(jnp.concatenate(mixed, axis=1), state, high)
    first = jnp.concatenate([own[:, :1] for own in lift], axis=1)
    last = jnp.concatenate([own[:, width - 1 :] for own in lift], axis=1)
    place = lax.axis_index("axial")
    inside = (place > 0, place < lax.axis_size("axial") - 1)
    before, after = [jnp.where(there, ref[...], 0.0) for there, ref in zip(inside, (before_ref, after_ref))]
    edge = mm_nt(lift[0], before, high) + mm_nt(lift[-1], after, high)
    edge = edge + mm_nt(first, sides_ref[chans:, :], high) + mm_nt(last, sides_ref[:chans, :], high)
    total = prod[:8] + mm_nt(jnp.concatenate(lift, axis=1), source, high)
    total = total - mm(prod[8:], jac_ref[...], high) + 0.5 * edge
    out = [jnp.concatenate([total[2 * i : 2 * i + 1], total[2 * i + 1 : 2 * i + 2]], axis=1) for i in range(seps // 2)]
    out.append(jnp.zeros((8 - seps // 2, lanes), jnp.float32))
    f_ref[...] = jnp.concatenate(out, axis=0)


def edges_kernel(state_ref, top_ref, bottom_ref, sides_ref):
    rows, cells = state_ref.shape[1:]
    top_ref[...] = state_ref[:, 0, :]
    bottom_ref[...] = state_ref[:, rows - 1, :]
    left = jnp.concatenate([state_ref[:, i, :1] for i in range(rows)], axis=1)
    right = jnp.concatenate([state_ref[:, i, cells - 1 :] for i in range(rows)], axis=1)
    sides_ref[...] = jnp.concatenate([left, right], axis=0)


def is_upper(level):
    return jnp.bitwise_and(jnp.right_shift(lax.axis_index(everywhere), level), 1) != 0


def order(upper, own, other):
    return jnp.where(upper, other, own), jnp.where(upper, own, other)


def first_kernel(own_ref, other_ref, sep_ref, ss_ref, inv_ref, xt2_ref, where_ref):
    seps = sep_ref.shape[1]
    c_of = lax.broadcasted_iota(jnp.int32, (8, seps), 0)
    own_c = c_of == lax.broadcasted_iota(jnp.int32, (8, seps), 1)
    where = jnp.max(jnp.where(own_c, sep_ref[...], -1), axis=1, keepdims=True)
    where_ref[...] = jnp.broadcast_to(where, (8, lanes)).astype(jnp.float32)
    half = own_ref.shape[0] // 2
    upper = is_upper(0)
    inverse = mm_tn(*factorize(own_ref[half:, half:] + other_ref[half:, half:], half // 3))
    inv_ref[...] = inverse
    _, os2 = order(upper, own_ref[:half, half:], other_ref[:half, half:])
    _, oo2 = order(upper, own_ref[:half, :half], other_ref[:half, :half])
    xt2 = mm(os2, inverse)
    xt2_ref[...] = xt2
    ss_ref[...] = pack_symmetric(oo2 - mm_nt(xt2, os2))


def factor_kernel(own_ref, other_ref, inv_ref):
    inv_ref[...] = mm_tn(*factorize(unpack_symmetric(own_ref[...] + other_ref[...]), own_ref.shape[0] // 3))


def shared_kernel(level, inv_ref, own_ref, other_ref, ss_ref, xt2_ref):
    half = inv_ref.shape[0]
    full = half * 3 // 2
    upper = is_upper(level)
    _, oo2 = order(upper, own_ref[:half, :], other_ref[:half, :])
    _, os2 = order(upper, own_ref[half : half + full, :], other_ref[half : half + full, :])
    os2 = unpack_full(os2)
    xt2 = mm(os2, inv_ref[...])
    xt2_ref[...] = xt2
    ss_ref[...] = oo2 - pack_symmetric(mm_nt(xt2, os2))


def split_rhs(upper, own_f, other_f):
    own, other = to_row(own_f), to_row(other_f)
    first, second = order(upper, own, other)
    half = own.shape[1] // 2
    return own[:, half:] + other[:, half:], jnp.concatenate([first[:, :half], second[:, :half]], axis=1)


def merge(upper, inv_ref, xt2_ref, os1, os2, own_f, other_f, xt_ref, z_ref):
    half = inv_ref.shape[0]
    shared, outer = split_rhs(upper, own_f, other_f)
    xt = mm(jnp.concatenate([os1, jnp.broadcast_to(shared, (8, half))], axis=0), inv_ref[...])
    xt_ref[:half, :] = xt[:half]
    xt_ref[half:, :] = xt2_ref[...]
    z_ref[...] = xt[half : half + 1]
    both = mm_nt(xt, jnp.concatenate([os1, os2], axis=0))
    return both[:half, :half], -both[:half, half:], outer - both[half : half + 1]


def put_rest(rest_ref, oo, cross, f):
    half = cross.shape[0]
    full = half * 3 // 2
    rest_ref[:half, :] = oo
    rest_ref[half : half + full, :] = pack_full(cross)
    rest_ref[half + full :, :] = from_row(f)


def first_rest_kernel(inv_ref, xt2_ref, own_ref, other_ref, own_f_ref, other_f_ref, rest_ref, xt_ref, z_ref):
    half = inv_ref.shape[0]
    upper = is_upper(0)
    os1, os2 = order(upper, own_ref[:half, half:], other_ref[:half, half:])
    oo1, _ = order(upper, own_ref[:half, :half], other_ref[:half, :half])
    less, cross, f = merge(upper, inv_ref, xt2_ref, os1, os2, own_f_ref[...], other_f_ref[...], xt_ref, z_ref)
    put_rest(rest_ref, pack_symmetric(oo1 - less), cross, f)


def unpacked(upper, own_ref, other_ref, half):
    full = half * 3 // 2
    oo1, oo2 = order(upper, own_ref[:half, :], other_ref[:half, :])
    os1, os2 = order(upper, own_ref[half : half + full, :], other_ref[half : half + full, :])
    return os1, os2, oo1, oo2, own_ref[half + full :, :], other_ref[half + full :, :]


def rest_kernel(level, inv_ref, xt2_ref, own_ref, other_ref, rest_ref, xt_ref, z_ref):
    upper = is_upper(level)
    os1, os2, oo1, _, own_f, other_f = unpacked(upper, own_ref, other_ref, inv_ref.shape[0])
    less, cross, f = merge(
        upper, inv_ref, xt2_ref, unpack_full(os1), unpack_full(os2), own_f, other_f, xt_ref, z_ref
    )
    put_rest(rest_ref, oo1 - pack_symmetric(less), cross, f)


def end_kernel(level, inv_ref, own_ref, other_ref, t_ref, xt_ref, z_ref, end_v_ref, end_r_ref, work_ref):
    half = inv_ref.shape[0]
    upper = is_upper(level)
    os1, os2, oo1, oo2, own_f, other_f = unpacked(upper, own_ref, other_ref, half)
    os1 = unpack_full(os1)
    xt1 = mm(os1, inv_ref[...])
    xt_ref[:half, :] = xt1
    piece = half // 3
    os2 = unpack_full(os2)
    done = {}

    def products(i):
        rows = slice(i * piece, (i + 1) * piece)
        xt_ref[half + i * piece : half + (i + 1) * piece, :] = mm(os2[rows], inv_ref[...])

    def crosses(i):
        rows = slice(i * piece, (i + 1) * piece)
        work_ref[rows, :] = mm_nt(os2[rows], xt_ref[...])

    def right():
        shared, outer = split_rhs(upper, own_f, other_f)
        z = mm(jnp.broadcast_to(shared, (8, half)), inv_ref[...])
        z_ref[...] = z[:1]
        done["f"] = outer - mm_nt(z, jnp.concatenate([os1, os2], axis=0))[:1]

    jobs = [functools.partial(products, i) for i in range(3)] + [functools.partial(crosses, i) for i in range(3)]
    g, r = factorize(unpack_symmetric(oo1) - mm_nt(xt1, os1), half // 2, jobs + [right])
    end_r_ref[...] = r
    f = done["f"]
    stacked = jnp.concatenate([-work_ref[:, :half], jnp.broadcast_to(f[:, :half], (8, half))], axis=0)
    vu = mm_nt(stacked, jnp.concatenate([g, r], axis=0))
    end_v_ref[...] = vu[:, :half]
    lost = mm_nt(vu[:, half:], vu[:half, :half])
    t_ref[:half, :] = oo2 - pack_symmetric(work_ref[:, half:] + lost[:half])
    t_ref[half:, :] = from_row(
        jnp.concatenate([f[:, half:] - lost[half : half + 1], jnp.zeros((1, half), jnp.float32)], axis=1)
    )


def compose_kernel(levels, end_v_ref, end_r_ref, *refs):
    half = end_r_ref.shape[0]
    out_ref = refs[-1]
    row = lax.broadcasted_iota(jnp.int32, (half + 8, half), 0)
    col = lax.broadcasted_iota(jnp.int32, (half + 8, half), 1)
    outer = mm(jnp.where(row < half, -end_v_ref[...], end_v_ref[...]), end_r_ref[...])
    answer = jnp.concatenate([outer, jnp.where(row == col, 1.0, 0.0)], axis=1)
    for level in reversed(range(levels)):
        xt_ref, z_ref = refs[2 * level : 2 * level + 2]
        inner = jnp.where(row >= half, z_ref[...], 0.0) - mm(answer, xt_ref[...])
        outer = jnp.where(is_upper(level), answer[:, half:], answer[:, :half])
        answer = jnp.concatenate([outer, inner], axis=1)
    out_ref[...] = answer


def solve_kernel(own_ref, other_ref, map_ref, out_ref):
    half = map_ref.shape[0] - 8
    width = map_ref.shape[1]
    total = own_ref[...] + other_ref[...]
    right = jnp.broadcast_to(to_row(total[half:])[:, :half], (8, half)).T
    pad = jnp.zeros((half, lanes - half % lanes - 8), jnp.float32)
    g, r = factorize(jnp.concatenate([unpack_symmetric(total[:half]), right, pad], axis=1), half // 2)
    shared = jnp.sum(g[:, half : half + 1] * r[:, :half], axis=0, keepdims=True)
    shared = jnp.broadcast_to(shared, (8, half)).T[:, :1]
    parts = jnp.broadcast_to(shared, (half, width)) * map_ref[:half, :]
    out_ref[...] = jnp.sum(parts, axis=0, keepdims=True) + map_ref[half : half + 1, :]


vmem = pl.BlockSpec(memory_space=pltpu.VMEM)


def call(kernel, name, shapes, micros, *operands, scratch=()):
    outs = tuple(jax.ShapeDtypeStruct(s, jnp.float32) for s in shapes)
    single = len(outs) == 1
    return pl.pallas_call(
        kernel,
        out_shape=outs[0] if single else outs,
        in_specs=[vmem] * len(operands),
        out_specs=vmem if single else tuple(vmem for _ in outs),
        scratch_shapes=[pltpu.VMEM(shape, jnp.float32) for shape in scratch],
        compiler_params=pltpu.CompilerParams(vmem_limit_bytes=32 << 20),
        cost_estimate=pl.CostEstimate(flops=int(micros * 1e9), bytes_accessed=0, transcendentals=0),
        name=name,
    )(*operands)


def partner(array, level):
    count = lax.axis_size(everywhere)
    return lax.ppermute(array, everywhere, [(i, i ^ 1 << level) for i in range(count)])


def halos(state):
    chans, rows, cells = state.shape
    axial, azim = lax.axis_size("axial"), lax.axis_size("azim")
    shapes = [(chans, cells), (chans, cells), (2 * chans, rows)]
    top, bottom, sides = call(edges_kernel, "edges", shapes, 0.5, state)
    up = [(i, (i + 1) % axial) for i in range(axial)]
    before = lax.ppermute(bottom, "axial", up)
    after = lax.ppermute(top, "axial", [(j, i) for i, j in up])
    around = [(i, (i + 1) % azim) for i in range(azim)]
    if azim == 2:
        sides = lax.ppermute(sides, "azim", around)
    else:
        left = lax.ppermute(sides[chans:], "azim", around)
        right = lax.ppermute(sides[:chans], "azim", [(j, i) for i, j in around])
        sides = jnp.concatenate([right, left], axis=0)
    return before, after, sides


def body(adjoint_state, adjoint_source, reaction_rate, jacobian, lifting, separator, leaf_schur):
    chans, rows, cells = adjoint_state.shape[1:]
    width = leaf_schur.shape[-1]
    half = width // 2
    full = half * 3 // 2
    levels = lax.axis_size(everywhere).bit_length() - 1
    rest_shapes = [(half + full + 8, lanes), (width, half), (1, half)]
    shared_shapes = [(half, lanes), (half, half)]

    schur = leaf_schur.reshape(width, width)
    other_schur = partner(schur, 0)
    state = adjoint_state.reshape(chans, rows, cells)
    edges = halos(state)
    ss, inverse, xt2, where = call(
        first_kernel,
        "factor_0",
        [(half, lanes), (half, half), (half, half), (8, lanes)],
        8.0,
        schur,
        other_schur,
        separator.reshape(1, -1),
    )
    other_ss = partner(ss, 1)
    f = call(
        leaf_kernel,
        "leaf_rhs",
        [(8, lanes)],
        2.3,
        where,
        ss,
        state,
        adjoint_source.reshape(chans, rows, cells),
        reaction_rate.reshape(rows, cells),
        jacobian.reshape(chans, chans),
        lifting.reshape(-1, rows, cells),
        *edges,
    )
    rest, xt, z = call(
        first_rest_kernel, "rest_0", rest_shapes, 0.05, inverse, xt2, schur, other_schur, f, partner(f, 0)
    )
    other_rest = partner(rest, 1)
    saved = [xt, z]
    for level in range(1, levels - 1):
        inverse = call(factor_kernel, f"factor_{level}", [(half, half)], 6.5, ss, other_ss)
        operands = (rest, other_rest)
        if level < levels - 2:
            ss, xt2 = call(
                functools.partial(shared_kernel, level), f"shared_{level}", shared_shapes, 1.5, inverse, *operands
            )
            other_ss = partner(ss, level + 1)
            rest, xt, z = call(
                functools.partial(rest_kernel, level), f"rest_{level}", rest_shapes, 0.05, inverse, xt2, *operands
            )
            other_rest = partner(rest, level + 1)
        else:
            end, xt, z, end_v, end_r = call(
                functools.partial(end_kernel, level),
                f"end_{level}",
                [(half + 8, lanes), (width, half), (1, half), (half + 8, half), (half, half)],
                9.5,
                inverse,
                *operands,
                scratch=[(half, width)],
            )
        saved += [xt, z]
    other_end = partner(end, levels - 1)
    composed = call(
        functools.partial(compose_kernel, levels - 1), "compose", [(half + 8, width)], 3.7, end_v, end_r, *saved
    )
    answer = call(solve_kernel, "solve", [(1, width)], 7.0, end, other_end, composed)
    return answer.reshape(1, 1, 1, width)


def solution(mesh):
    in_specs = (
        P("bank", None, "axial", "azim"),
        P("bank", None, "axial", "azim"),
        P("bank", "axial", "azim"),
        P("bank", None, None),
        P("bank", None, "axial", "azim"),
        P("axial", "azim", "bank", None),
        P("axial", "azim", "bank", None, None),
    )
    out_specs = P("axial", "azim", "bank", None)
    return jax.shard_map(body, mesh=mesh, in_specs=in_specs, out_specs=out_specs, check_vma=False)
```

time: 73.5 us -> 68.6 us (0.933)
  starting transfers between devices: 19.4 us -> 15.9 us
  Pallas kernels: 44.8 us -> 42.7 us
  waiting for transfers between devices: 7.24 us -> 8.52 us
    ppermute x9, starting transfers between devices: 12.1 us -> 8.63 us  [partner(): lax.ppermute(array, everywhere, [(i, i ^ 1 << level) for i in range(count)])]
    pallas_call x14, Pallas kernels: 44.8 us -> 42.7 us  [call(): pl.pallas_call(kernel, out_shape=outs[0] if single else outs, in_specs=[v...]
    ppermute x1, starting transfers between devices: 4.4 us -> 2.54 us  [halos(): before = lax.ppermute(bottom, 'axial', up)]
    ppermute x1, starting transfers between devices: 1.29 us -> 3.1 us  [halos(): after = lax.ppermute(top, 'axial', [(j, i) for i, j in up])]
    ppermute x9, waiting for transfers between devices: 7.23 us -> 8.51 us  [partner(): lax.ppermute(array, everywhere, [(i, i ^ 1 << level) for i in range(count)])]
  transfers between devices with their start and end apart: 12 -> 12, of which waited for: 5 -> 5; matrix products, arithmetic and copies ran while one was open for 0% -> 0% of each run, Pallas kernels for 39% -> 42%
where the time goes in v1:
time: 68.6 us; the launch traced here: 68.5 us
  Pallas kernels  42.7 us (62%)
  starting transfers between devices  15.9 us (23%)
  waiting for transfers between devices  8.52 us (12%)
  local copies, waits for them, and re-layouts  1.08 us (2%)
    pallas_call x14, Pallas kernels, call(): pl.pallas_call(kernel, out_shape=outs[0] if single else outs, in_specs=[v...  42.7 us
    ppermute x9, starting transfers between devices, partner(): lax.ppermute(array, everywhere, [(i, i ^ 1 << level) for i in range(count)])  8.63 us
    ppermute x9, waiting for transfers between devices, partner(): lax.ppermute(array, everywhere, [(i, i ^ 1 << level) for i in range(count)])  8.51 us
    ppermute x1, starting transfers between devices, halos(): after = lax.ppermute(top, 'axial', [(j, i) for i, j in up])  3.1 us
    ppermute x1, starting transfers between devices, halos(): before = lax.ppermute(bottom, 'axial', up)  2.54 us
    ppermute x1, starting transfers between devices, halos(): sides = lax.ppermute(sides, 'azim', around)  1.66 us
  transfers between devices with their start and end apart: 12, of which 5 were waited for; matrix products, arithmetic and copies ran while one was open for 0% of the time, Pallas kernels for 42%

profile of v1, /device:TPU:0, one launch (start us, length us, event | category | flops | bytes accessed | tf_op | source)
XLA Modules:
  0.0 68.5 jit_solution(12783057475994450069)
XLA Ops:
  0.0 0.5 collective-permute-start
  0.5 0.0 copy-start.1
  0.5 1.0 %copy-done.1 = f32[1,64,8,256]{3,2,1,0:T(8,128)S(1)} copy-done((f32[1,64,8,256]{3,2,1,0:T(8,128)S(1)}, f32[1,64,8,256]{3,2,1,0:T(8,128)}, u32[]{:S(2)}) %copy-start.1) | copy-done | bytes 524312
  1.5 0.0 copy-start
  1.5 0.3 edges.1
  1.8 2.5 %collective-permute-start.2 = (f32[64,256]{1,0:T(8,128)S(1)}, f32[64,256]{1,0:T(8,128)S(1)}, u32[]{:S(2)}, u32[]{:S(2)}) collective-permute-start(f32[64,256]{1,0:T(8,128)S(1)} %get-tuple-element.34), channel_id=1, source_target_pairs={{0,4},{4,8},{8,12},{12,16},{16,20},{20,24},{24,28},{28,0},{1,5},{5... | collective-permute-start | bytes 196616 | tf_op jit(solution)/shard_map/ppermute | solution.py:412
  4.3 3.1 %collective-permute-start.3 = (f32[64,256]{1,0:T(8,128)S(1)}, f32[64,256]{1,0:T(8,128)S(1)}, u32[]{:S(2)}, u32[]{:S(2)}) collective-permute-start(f32[64,256]{1,0:T(8,128)S(1)} %get-tuple-element.35), channel_id=1, source_target_pairs={{4,0},{8,4},{12,8},{16,12},{20,16},{24,20},{28,24},{0,28},{5,1},{9... | collective-permute-start | bytes 196616 | tf_op jit(solution)/shard_map/ppermute | solution.py:413
  7.4 0.0 copy-start.7
  7.4 1.7 %collective-permute-start.4 = (f32[128,8]{1,0:T(8,128)S(1)}, f32[128,8]{1,0:T(8,128)S(1)}, u32[]{:S(2)}, u32[]{:S(2)}) collective-permute-start(f32[128,8]{1,0:T(8,128)S(1)} %get-tuple-element.36), channel_id=1, source_target_pairs={{0,2},{2,0},{1,3},{3,1},{4,6},{6,4},{5,7},{7,5},{8,10},{10,8},{9,1... | collective-permute-start | bytes 12296 | tf_op jit(solution)/shard_map/ppermute | solution.py:416
  9.1 0.0 collective-permute-done.other_ref
  9.1 0.0 copy-done
  9.1 0.0 copy-done.7
  9.1 0.0 copy-start.2
  9.1 0.0 copy-start.3
  9.1 0.0 copy-start.4
  9.1 0.0 copy-start.5
  9.2 5.8 %factor_0.1 = (f32[192,128]{1,0:T(8,128)S(1)}, f32[192,192]{1,0:T(8,128)S(1)}, f32[192,192]{1,0:T(8,128)S(1)}, f32[8,128]{1,0:T(8,128)S(1)}) custom-call(f32[384,384]{1,0:T(8,128)S(1)} %bitcast.9, f32[384,384]{1,0:T(8,128)S(1)} %collective-permute-done.other_ref, s32[1,6]{1,0:T(1,128)S(1)} %bitcast.17), custom_call_target="tpu_custom_call" | custom-call | flops 8000000000 | tf_op jit(solution)/shard_map/factor_0/pallas_call | solution.py:389
  15.0 0.0 copy-start.6
  15.0 0.7 collective-permute-start.1
  15.7 0.0 collective-permute-done.4.sides_ref
  15.7 0.0 collective-permute-done.2.before_ref
  15.7 0.0 collective-permute-done.3.after_ref
  15.7 0.0 copy-done.2
  15.7 0.0 copy-done.3
  15.7 0.0 copy-done.4
  15.7 0.0 copy-done.5
  15.7 0.0 copy-done.6
  15.8 0.9 %leaf_rhs.1.own_f_ref = f32[8,128]{1,0:T(8,128)S(1)} custom-call(f32[8,128]{1,0:T(8,128)S(1)} %get-tuple-element.33.where_ref, f32[192,128]{1,0:T(8,128)S(1)} %get-tuple-element.30.own_ref.after_this_ref, f32[64,8,256]{2,1,0:T(8,128)S(1)} %bitcast.12, f32[64,8,256]{2,1,0:T(8,128)S(1)} %bitcast.13, f32[8,256]{1,0:T(8,128)S(1)} %bitcast.16, ...), custom_call_target="tpu_custom_call" | custom-call | flops 2300000000 | tf_op jit(solution)/shard_map/leaf_rhs/pallas_call | solution.py:389
  16.6 0.0 collective-permute-start.5
  16.6 1.2 %collective-permute-done.5.other_f_ref = f32[8,128]{1,0:T(8,128)S(1)} collective-permute-done((f32[8,128]{1,0:T(8,128)S(1)}, f32[8,128]{1,0:T(8,128)S(1)}, u32[]{:S(2)}, u32[]{:S(2)}) %collective-permute-start.5) | collective-permute-done | bytes 4128 | tf_op jit(solution)/shard_map/ppermute | solution.py:403
  17.8 1.1 %rest_0.1 = (f32[488,128]{1,0:T(8,128)S(1)}, f32[384,192]{1,0:T(8,128)S(1)}, f32[1,192]{1,0:T(1,128)S(1)}) custom-call(f32[192,192]{1,0:T(8,128)S(1)} %get-tuple-element.31.inv_ref, f32[192,192]{1,0:T(8,128)S(1)} %get-tuple-element.32.xt2_ref, f32[384,384]{1,0:T(8,128)S(1)} %bitcast.10, f32[384,384]{1,0:T(8,128)S(1)} %collective-permute-done.other_ref, ...), custom_call_target="tpu_custom_call" | custom-call | flops 50000000 | tf_op jit(solution)/shard_map/rest_0/pallas_call | solution.py:389
  18.9 1.4 %collective-permute-start.6 = (f32[488,128]{1,0:T(8,128)S(1)}, f32[488,128]{1,0:T(8,128)S(1)}, u32[]{:S(2)}, u32[]{:S(2)}) collective-permute-start(f32[488,128]{1,0:T(8,128)S(1)} %get-tuple-element.37.own_ref), channel_id=1, source_target_pairs={{0,2},{1,3},{2,0},{3,1},{4,6},{5,7},{6,4},{7,5},{8,10},{9,11},{10,... | collective-permute-start | bytes 749576 | tf_op jit(solution)/shard_map/ppermute | solution.py:403
  20.3 0.0 collective-permute-done.1.other_ref
  20.3 5.0 %factor_1.1.inv_ref = f32[192,192]{1,0:T(8,128)S(1)} custom-call(f32[192,128]{1,0:T(8,128)S(1)} %get-tuple-element.30.own_ref.after_this_ref, f32[192,128]{1,0:T(8,128)S(1)} %collective-permute-done.1.other_ref), custom_call_target="tpu_custom_call" | custom-call | flops 6499999744 | tf_op jit(solution)/shard_map/factor_1/pallas_call | solution.py:389
  25.3 1.7 %collective-permute-done.6.other_ref = f32[488,128]{1,0:T(8,128)S(1)} collective-permute-done((f32[488,128]{1,0:T(8,128)S(1)}, f32[488,128]{1,0:T(8,128)S(1)}, u32[]{:S(2)}, u32[]{:S(2)}) %collective-permute-start.6) | collective-permute-done | bytes 249888 | tf_op jit(solution)/shard_map/ppermute | solution.py:403
  27.0 0.9 %shared_1.1 = (f32[192,128]{1,0:T(8,128)S(1)}, f32[192,192]{1,0:T(8,128)S(1)}) custom-call(f32[192,192]{1,0:T(8,128)S(1)} %factor_1.1.inv_ref, f32[488,128]{1,0:T(8,128)S(1)} %get-tuple-element.37.own_ref, f32[488,128]{1,0:T(8,128)S(1)} %collective-permute-done.6.other_ref), custom_call_target="tpu_custom_call" | custom-call | flops 1500000000 | tf_op jit(solution)/shard_map/shared_1/pallas_call | solution.py:389
  28.0 0.1 collective-permute-start.7
  28.0 1.1 %rest_1.1 = (f32[488,128]{1,0:T(8,128)S(1)}, f32[384,192]{1,0:T(8,128)S(1)}, f32[1,192]{1,0:T(1,128)S(1)}) custom-call(f32[192,192]{1,0:T(8,128)S(1)} %factor_1.1.inv_ref, f32[192,192]{1,0:T(8,128)S(1)} %get-tuple-element.39.xt2_ref, f32[488,128]{1,0:T(8,128)S(1)} %get-tuple-element.37.own_ref, f32[488,128]{1,0:T(8,128)S(1)} %collective-permute-done.6.other_ref), custom_call_target="tpu_custom_call" | custom-call | flops 50000000 | tf_op jit(solution)/shard_map/rest_1/pallas_call | solution.py:389
  29.1 2.0 %collective-permute-start.8 = (f32[488,128]{1,0:T(8,128)S(1)}, f32[488,128]{1,0:T(8,128)S(1)}, u32[]{:S(2)}, u32[]{:S(2)}) collective-permute-start(f32[488,128]{1,0:T(8,128)S(1)} %get-tuple-element.40.own_ref), channel_id=1, source_target_pairs={{0,4},{1,5},{2,6},{3,7},{4,0},{5,1},{6,2},{7,3},{8,12},{9,13},{10,... | collective-permute-start | bytes 749576 | tf_op jit(solution)/shard_map/ppermute | solution.py:403
  31.1 2.5 %collective-permute-done.7.other_ref = f32[192,128]{1,0:T(8,128)S(1)} collective-permute-done((f32[192,128]{1,0:T(8,128)S(1)}, f32[192,128]{1,0:T(8,128)S(1)}, u32[]{:S(2)}, u32[]{:S(2)}) %collective-permute-start.7) | collective-permute-done | bytes 98336 | tf_op jit(solution)/shard_map/ppermute | solution.py:403
  33.6 5.1 %factor_2.1.inv_ref = f32[192,192]{1,0:T(8,128)S(1)} custom-call(f32[192,128]{1,0:T(8,128)S(1)} %get-tuple-element.38.own_ref, f32[192,128]{1,0:T(8,128)S(1)} %collective-permute-done.7.other_ref), custom_call_target="tpu_custom_call" | custom-call | flops 6499999744 | tf_op jit(solution)/shard_map/factor_2/pallas_call | solution.py:389
  38.8 0.0 collective-permute-done.8.other_ref
  38.8 0.9 %shared_2.1 = (f32[192,128]{1,0:T(8,128)S(1)}, f32[192,192]{1,0:T(8,128)S(1)}) custom-call(f32[192,192]{1,0:T(8,128)S(1)} %factor_2.1.inv_ref, f32[488,128]{1,0:T(8,128)S(1)} %get-tuple-element.40.own_ref, f32[488,128]{1,0:T(8,128)S(1)} %collective-permute-done.8.other_ref), custom_call_target="tpu_custom_call" | custom-call | flops 1500000000 | tf_op jit(solution)/shard_map/shared_2/pallas_call | solution.py:389
  39.7 0.1 collective-permute-start.9
  39.8 1.1 %rest_2.1 = (f32[488,128]{1,0:T(8,128)S(1)}, f32[384,192]{1,0:T(8,128)S(1)}, f32[1,192]{1,0:T(1,128)S(1)}) custom-call(f32[192,192]{1,0:T(8,128)S(1)} %factor_2.1.inv_ref, f32[192,192]{1,0:T(8,128)S(1)} %get-tuple-element.42.xt2_ref, f32[488,128]{1,0:T(8,128)S(1)} %get-tuple-element.40.own_ref, f32[488,128]{1,0:T(8,128)S(1)} %collective-permute-done.8.other_ref), custom_call_target="tpu_custom_call" | custom-call | flops 50000000 | tf_op jit(solution)/shard_map/rest_2/pallas_call | solution.py:389
  40.8 2.0 %collective-permute-start.10 = (f32[488,128]{1,0:T(8,128)S(1)}, f32[488,128]{1,0:T(8,128)S(1)}, u32[]{:S(2)}, u32[]{:S(2)}) collective-permute-start(f32[488,128]{1,0:T(8,128)S(1)} %get-tuple-element.43.own_ref), channel_id=1, source_target_pairs={{0,8},{1,9},{2,10},{3,11},{4,12},{5,13},{6,14},{7,15},{8,0},{9,1},... | collective-permute-start | bytes 749576 | tf_op jit(solution)/shard_map/ppermute | solution.py:403
  42.9 1.6 %collective-permute-done.9.other_ref = f32[192,128]{1,0:T(8,128)S(1)} collective-permute-done((f32[192,128]{1,0:T(8,128)S(1)}, f32[192,128]{1,0:T(8,128)S(1)}, u32[]{:S(2)}, u32[]{:S(2)}) %collective-permute-start.9) | collective-permute-done | bytes 98336 | tf_op jit(solution)/shard_map/ppermute | solution.py:403
  44.5 5.0 %factor_3.1.inv_ref = f32[192,192]{1,0:T(8,128)S(1)} custom-call(f32[192,128]{1,0:T(8,128)S(1)} %get-tuple-element.41.own_ref, f32[192,128]{1,0:T(8,128)S(1)} %collective-permute-done.9.other_ref), custom_call_target="tpu_custom_call" | custom-call | flops 6499999744 | tf_op jit(solution)/shard_map/factor_3/pallas_call | solution.py:389
  49.4 0.0 collective-permute-done.10.other_ref
  49.5 7.1 %end_3.1 = (f32[200,128]{1,0:T(8,128)S(1)}, f32[384,192]{1,0:T(8,128)S(1)}, f32[1,192]{1,0:T(1,128)S(1)}, f32[200,192]{1,0:T(8,128)S(1)}, f32[192,192]{1,0:T(8,128)S(1)}) custom-call(f32[192,192]{1,0:T(8,128)S(1)} %factor_3.1.inv_ref, f32[488,128]{1,0:T(8,128)S(1)} %get-tuple-element.43.own_ref, f32[488,128]{1,0:T(8,128)S(1)} %collective-permute-done.10.other_ref), custom_call_target="tpu_custom_call" | custom-call | flops 9500000256 | tf_op jit(solution)/shard_map/end_3/pallas_call | solution.py:389
  56.5 1.8 %collective-permute-start.11 = (f32[200,128]{1,0:T(8,128)S(1)}, f32[200,128]{1,0:T(8,128)S(1)}, u32[]{:S(2)}, u32[]{:S(2)}) collective-permute-start(f32[200,128]{1,0:T(8,128)S(1)} %get-tuple-element.44.own_ref), channel_id=1, source_target_pairs={{0,16},{1,17},{2,18},{3,19},{4,20},{5,21},{6,22},{7,23},{8,24},{9,... | collective-permute-start | bytes 307208 | tf_op jit(solution)/shard_map/ppermute | solution.py:403
  58.3 3.4 %compose.1.map_ref = f32[200,384]{1,0:T(8,128)S(1)} custom-call(f32[200,192]{1,0:T(8,128)S(1)} %get-tuple-element.45.end_v_ref, f32[192,192]{1,0:T(8,128)S(1)} %get-tuple-element.46.end_r_ref, f32[384,192]{1,0:T(8,128)S(1)} %get-tuple-element.47.refs_0_, f32[1,192]{1,0:T(1,128)S(1)} %get-tuple-element.48.refs_1_, f32[384,192]{1,0:T(8,128)S(1)} %get-tuple-element.49.refs_2_, ...), custom_call_target="tpu_custom_call" | custom-call | flops 3700000000 | tf_op jit(solution)/shard_map/compose/pallas_call | solution.py:389
  61.8 1.5 %collective-permute-done.11.other_ref = f32[200,128]{1,0:T(8,128)S(1)} collective-permute-done((f32[200,128]{1,0:T(8,128)S(1)}, f32[200,128]{1,0:T(8,128)S(1)}, u32[]{:S(2)}, u32[]{:S(2)}) %collective-permute-start.11) | collective-permute-done | bytes 102432 | tf_op jit(solution)/shard_map/ppermute | solution.py:403
  63.3 5.2 %solve.1 = f32[1,384]{1,0:T(1,128)} custom-call(f32[200,128]{1,0:T(8,128)S(1)} %get-tuple-element.44.own_ref, f32[200,128]{1,0:T(8,128)S(1)} %collective-permute-done.11.other_ref, f32[200,384]{1,0:T(8,128)S(1)} %compose.1.map_ref), custom_call_target="tpu_custom_call" | custom-call | flops 7000000000 | tf_op jit(solution)/shard_map/solve/pallas_call | solution.py:389
Async XLA Ops:
  0.0 9.1 %collective-permute-start = (f32[384,384]{1,0:T(8,128)}, f32[384,384]{1,0:T(8,128)S(1)}, u32[]{:S(2)}, u32[]{:S(2)}) collective-permute-start(f32[384,384]{1,0:T(8,128)} %bitcast.8), channel_id=1, source_target_pairs={{0,1},{1,0},{2,3},{3,2},{4,5},{5,4},{6,7},{7,6},{8,9},{9,8},{10,11... | collective-permute-start | bytes 1769480 | tf_op jit(solution)/shard_map/ppermute | solution.py:403
  0.5 1.0 %copy-start.1 = (f32[1,64,8,256]{3,2,1,0:T(8,128)S(1)}, f32[1,64,8,256]{3,2,1,0:T(8,128)}, u32[]{:S(2)}) copy-start(f32[1,64,8,256]{3,2,1,0:T(8,128)} %param.7) | copy-start | bytes 1572868
  1.5 7.6 %copy-start = (f32[1,1,1,384,384]{4,3,2,1,0:T(8,128)S(1)}, f32[1,1,1,384,384]{4,3,2,1,0:T(8,128)}, u32[]{:S(2)}) copy-start(f32[1,1,1,384,384]{4,3,2,1,0:T(8,128)} %param.13) | copy-start | bytes 1769476
  1.8 13.9 %collective-permute-start.2 = (f32[64,256]{1,0:T(8,128)S(1)}, f32[64,256]{1,0:T(8,128)S(1)}, u32[]{:S(2)}, u32[]{:S(2)}) collective-permute-start(f32[64,256]{1,0:T(8,128)S(1)} %get-tuple-element.34), channel_id=1, source_target_pairs={{0,4},{4,8},{8,12},{12,16},{16,20},{20,24},{24,28},{28,0},{1,5},{5... | collective-permute-start | bytes 196616 | tf_op jit(solution)/shard_map/ppermute | solution.py:412
  4.3 11.4 %collective-permute-start.3 = (f32[64,256]{1,0:T(8,128)S(1)}, f32[64,256]{1,0:T(8,128)S(1)}, u32[]{:S(2)}, u32[]{:S(2)}) collective-permute-start(f32[64,256]{1,0:T(8,128)S(1)} %get-tuple-element.35), channel_id=1, source_target_pairs={{4,0},{8,4},{12,8},{16,12},{20,16},{24,20},{28,24},{0,28},{5,1},{9... | collective-permute-start | bytes 196616 | tf_op jit(solution)/shard_map/ppermute | solution.py:413
  7.4 1.7 %copy-start.7 = (s32[1,1,1,6]{3,2,1,0:T(1,128)S(1)}, s32[1,1,1,6]{3,2,1,0:T(1,128)}, u32[]{:S(2)}) copy-start(s32[1,1,1,6]{3,2,1,0:T(1,128)} %param.12) | copy-start | bytes 76
  7.4 8.3 %collective-permute-start.4 = (f32[128,8]{1,0:T(8,128)S(1)}, f32[128,8]{1,0:T(8,128)S(1)}, u32[]{:S(2)}, u32[]{:S(2)}) collective-permute-start(f32[128,8]{1,0:T(8,128)S(1)} %get-tuple-element.36), channel_id=1, source_target_pairs={{0,2},{2,0},{1,3},{3,1},{4,6},{6,4},{5,7},{7,5},{8,10},{10,8},{9,1... | collective-permute-start | bytes 12296 | tf_op jit(solution)/shard_map/ppermute | solution.py:416
  9.1 6.6 %copy-start.2 = (f32[1,64,8,256]{3,2,1,0:T(8,128)S(1)}, f32[1,64,8,256]{3,2,1,0:T(8,128)}, u32[]{:S(2)}) copy-start(f32[1,64,8,256]{3,2,1,0:T(8,128)} %param.7) | copy-start | bytes 1572868
  9.1 6.6 %copy-start.3 = (f32[1,64,8,256]{3,2,1,0:T(8,128)S(1)}, f32[1,64,8,256]{3,2,1,0:T(8,128)}, u32[]{:S(2)}) copy-start(f32[1,64,8,256]{3,2,1,0:T(8,128)} %param.8) | copy-start | bytes 1572868
  9.1 6.6 %copy-start.4 = (f32[1,6,8,256]{3,2,1,0:T(8,128)S(1)}, f32[1,6,8,256]{3,2,1,0:T(8,128)}, u32[]{:S(2)}) copy-start(f32[1,6,8,256]{3,2,1,0:T(8,128)} %param.11) | copy-start | bytes 147460
  9.1 6.6 %copy-start.5 = (f32[1,64,64]{2,1,0:T(8,128)S(1)}, f32[1,64,64]{2,1,0:T(8,128)}, u32[]{:S(2)}) copy-start(f32[1,64,64]{2,1,0:T(8,128)} %param.10) | copy-start | bytes 49156
  15.0 0.7 %copy-start.6 = (f32[1,8,256]{2,1,0:T(8,128)S(1)}, f32[1,8,256]{2,1,0:T(8,128)}, u32[]{:S(2)}) copy-start(f32[1,8,256]{2,1,0:T(8,128)} %param.9) | copy-start | bytes 24580
  15.0 5.3 %collective-permute-start.1 = (f32[192,128]{1,0:T(8,128)S(1)}, f32[192,128]{1,0:T(8,128)S(1)}, u32[]{:S(2)}, u32[]{:S(2)}) collective-permute-start(f32[192,128]{1,0:T(8,128)S(1)} %get-tuple-element.30.own_ref.after_this_ref), channel_id=1, source_target_pairs={{0,2},{1,3},{2,0},{3,1},{4,6},{5,7},{6,4},{7,5},{8,10},{9,11},{10,... | collective-permute-start | bytes 294920 | tf_op jit(solution)/shard_map/ppermute | solution.py:403
  16.6 1.2 %collective-permute-start.5 = (f32[8,128]{1,0:T(8,128)S(1)}, f32[8,128]{1,0:T(8,128)S(1)}, u32[]{:S(2)}, u32[]{:S(2)}) collective-permute-start(f32[8,128]{1,0:T(8,128)S(1)} %leaf_rhs.1.own_f_ref), channel_id=1, source_target_pairs={{0,1},{1,0},{2,3},{3,2},{4,5},{5,4},{6,7},{7,6},{8,9},{9,8},{10,11... | collective-permute-start | bytes 12296 | tf_op jit(solution)/shard_map/ppermute | solution.py:403
  18.9 8.2 %collective-permute-start.6 = (f32[488,128]{1,0:T(8,128)S(1)}, f32[488,128]{1,0:T(8,128)S(1)}, u32[]{:S(2)}, u32[]{:S(2)}) collective-permute-start(f32[488,128]{1,0:T(8,128)S(1)} %get-tuple-element.37.own_ref), channel_id=1, source_target_pairs={{0,2},{1,3},{2,0},{3,1},{4,6},{5,7},{6,4},{7,5},{8,10},{9,11},{10,... | collective-permute-start | bytes 749576 | tf_op jit(solution)/shard_map/ppermute | solution.py:403
  28.0 5.7 %collective-permute-start.7 = (f32[192,128]{1,0:T(8,128)S(1)}, f32[192,128]{1,0:T(8,128)S(1)}, u32[]{:S(2)}, u32[]{:S(2)}) collective-permute-start(f32[192,128]{1,0:T(8,128)S(1)} %get-tuple-element.38.own_ref), channel_id=1, source_target_pairs={{0,4},{1,5},{2,6},{3,7},{4,0},{5,1},{6,2},{7,3},{8,12},{9,13},{10,... | collective-permute-start | bytes 294920 | tf_op jit(solution)/shard_map/ppermute | solution.py:403
  29.1 9.7 %collective-permute-start.8 = (f32[488,128]{1,0:T(8,128)S(1)}, f32[488,128]{1,0:T(8,128)S(1)}, u32[]{:S(2)}, u32[]{:S(2)}) collective-permute-start(f32[488,128]{1,0:T(8,128)S(1)} %get-tuple-element.40.own_ref), channel_id=1, source_target_pairs={{0,4},{1,5},{2,6},{3,7},{4,0},{5,1},{6,2},{7,3},{8,12},{9,13},{10,... | collective-permute-start | bytes 749576 | tf_op jit(solution)/shard_map/ppermute | solution.py:403
  39.7 4.8 %collective-permute-start.9 = (f32[192,128]{1,0:T(8,128)S(1)}, f32[192,128]{1,0:T(8,128)S(1)}, u32[]{:S(2)}, u32[]{:S(2)}) collective-permute-start(f32[192,128]{1,0:T(8,128)S(1)} %get-tuple-element.41.own_ref), channel_id=1, source_target_pairs={{0,8},{1,9},{2,10},{3,11},{4,12},{5,13},{6,14},{7,15},{8,0},{9,1},... | collective-permute-start | bytes 294920 | tf_op jit(solution)/shard_map/ppermute | solution.py:403
  40.8 8.6 %collective-permute-start.10 = (f32[488,128]{1,0:T(8,128)S(1)}, f32[488,128]{1,0:T(8,128)S(1)}, u32[]{:S(2)}, u32[]{:S(2)}) collective-permute-start(f32[488,128]{1,0:T(8,128)S(1)} %get-tuple-element.43.own_ref), channel_id=1, source_target_pairs={{0,8},{1,9},{2,10},{3,11},{4,12},{5,13},{6,14},{7,15},{8,0},{9,1},... | collective-permute-start | bytes 749576 | tf_op jit(solution)/shard_map/ppermute | solution.py:403
  56.5 6.7 %collective-permute-start.11 = (f32[200,128]{1,0:T(8,128)S(1)}, f32[200,128]{1,0:T(8,128)S(1)}, u32[]{:S(2)}, u32[]{:S(2)}) collective-permute-start(f32[200,128]{1,0:T(8,128)S(1)} %get-tuple-element.44.own_ref), channel_id=1, source_target_pairs={{0,16},{1,17},{2,18},{3,19},{4,20},{5,21},{6,22},{7,23},{8,24},{9,... | collective-permute-start | bytes 307208 | tf_op jit(solution)/shard_map/ppermute | solution.py:403

commit v2 on v1

--- a/solution.py
+++ b/solution.py
@@ -138,19 +138,47 @@
 
 def pack_symmetric(m):
     third = m.shape[0] // 3
-    low = jnp.concatenate([m[:third, 2 * third :], m[2 * third :, 2 * third :]], axis=1)
-    return jnp.concatenate([m[:third, : 2 * third], m[third : 2 * third, third:], low], axis=0)
+    one, two, three = [slice(i * third, (i + 1) * third) for i in range(3)]
+    row = lax.broadcasted_iota(jnp.int32, (third, third), 0)
+    col = lax.broadcasted_iota(jnp.int32, (third, third), 1)
+    second = m[two, two]
+    last = m[three, three]
+    diagonal = jnp.sum(jnp.where(row == col, second, 0.0), axis=0, keepdims=True)
+    tail = jnp.concatenate([diagonal, jnp.zeros((1, lanes - third), jnp.float32)], axis=1)
+    parts = [
+        jnp.concatenate([jnp.where(row >= col, m[one, one], second), m[one, two]], axis=1),
+        jnp.concatenate([m[one, three], m[two, three]], axis=1),
+        jnp.concatenate([last[: third // 2], last[third // 2 :]], axis=1),
+        jnp.concatenate([tail, jnp.zeros((7, lanes), jnp.float32)], axis=0),
+    ]
+    return jnp.concatenate(parts, axis=0)
 
 
 def unpack_symmetric(p):
-    third = p.shape[0] // 3
-    top, mid, low = p[:third], p[third : 2 * third], p[2 * third :]
+    third = lanes // 2
+    row = lax.broadcasted_iota(jnp.int32, (third, third), 0)
+    col = lax.broadcasted_iota(jnp.int32, (third, third), 1)
+    shared, upper = p[:third, :third], p[:third, third:]
+    turned = shared.T
+    right, mid = p[third : 2 * third, :third], p[third : 2 * third, third:]
+    start = 2 * third
+    last = p[start : start + third // 2]
+    last = jnp.concatenate([last[:, :third], last[:, third:]], axis=0)
+    tail = start + third // 2
+    first = jnp.where(row >= col, shared, turned)
+    second = jnp.where(row == col, p[tail : tail + 1, :third], jnp.where(row < col, shared, turned))
     rows = [
-        jnp.concatenate([top, low[:, :third]], axis=1),
-        jnp.concatenate([top[:, third:].T, mid], axis=1),
-        jnp.concatenate([low[:, :third].T, mid[:, third:].T, low[:, third:]], axis=1),
+        jnp.concatenate([first, upper, right], axis=1),
+        jnp.concatenate([upper.T, second, mid], axis=1),
+        jnp.concatenate([right.T, mid.T, last], axis=1),
     ]
     return jnp.concatenate(rows, axis=0)
+
+
+def with_rhs(packed, f):
+    size = packed.shape[0]
+    row = lax.broadcasted_iota(jnp.int32, (8, lanes), 0)
+    return jnp.concatenate([packed[: size - 8], jnp.where(row == 0, packed[size - 8 :], from_row(f))], axis=0)
 
 
 def pack_full(m):
@@ -167,12 +195,13 @@
 
 
 def to_row(f):
-    return jnp.concatenate([f[i : i + 1] for i in range(3)], axis=1)
+    return jnp.concatenate([f[i : i + 1] for i in range(1, 4)], axis=1)
 
 
 def from_row(row):
     parts = [row[:, i * lanes : (i + 1) * lanes] for i in range(3)]
-    return jnp.concatenate(parts + [jnp.zeros((5, lanes), jnp.float32)], axis=0)
+    zeros = jnp.zeros((4, lanes), jnp.float32)
+    return jnp.concatenate([zeros[:1], *parts, zeros], axis=0)
 
 
 def leaf_kernel(where_ref, after_this_ref, state_ref, source_ref, rate_ref, jac_ref, lift_ref, before_ref, after_ref, sides_ref, f_ref):
@@ -207,9 +236,7 @@
     edge = edge + mm_nt(first, sides_ref[chans:, :], high) + mm_nt(last, sides_ref[:chans, :], high)
     total = prod[:8] + mm_nt(jnp.concatenate(lift, axis=1), source, high)
     total = total - mm(prod[8:], jac_ref[...], high) + 0.5 * edge
-    out = [jnp.concatenate([total[2 * i : 2 * i + 1], total[2 * i + 1 : 2 * i + 2]], axis=1) for i in range(seps // 2)]
-    out.append(jnp.zeros((8 - seps // 2, lanes), jnp.float32))
-    f_ref[...] = jnp.concatenate(out, axis=0)
+    f_ref[...] = from_row(jnp.concatenate([total[i : i + 1] for i in range(seps)], axis=1))
 
 
 def edges_kernel(state_ref, top_ref, bottom_ref, sides_ref):
@@ -247,15 +274,14 @@
 
 
 def factor_kernel(own_ref, other_ref, inv_ref):
-    inv_ref[...] = mm_tn(*factorize(unpack_symmetric(own_ref[...] + other_ref[...]), own_ref.shape[0] // 3))
+    inv_ref[...] = mm_tn(*factorize(unpack_symmetric(own_ref[...] + other_ref[...]), inv_ref.shape[0] // 3))
 
 
 def shared_kernel(level, inv_ref, own_ref, other_ref, ss_ref, xt2_ref):
-    half = inv_ref.shape[0]
-    full = half * 3 // 2
     upper = is_upper(level)
-    _, oo2 = order(upper, own_ref[:half, :], other_ref[:half, :])
-    _, os2 = order(upper, own_ref[half : half + full, :], other_ref[half : half + full, :])
+    size = ss_ref.shape[0]
+    _, oo2 = order(upper, own_ref[:size, :], other_ref[:size, :])
+    _, os2 = order(upper, own_ref[size:, :], other_ref[size:, :])
     os2 = unpack_full(os2)
     xt2 = mm(os2, inv_ref[...])
     xt2_ref[...] = xt2
@@ -280,28 +306,41 @@
     return both[:half, :half], -both[:half, half:], outer - both[half : half + 1]
 
 
-def put_rest(rest_ref, oo, cross, f):
-    half = cross.shape[0]
-    full = half * 3 // 2
-    rest_ref[:half, :] = oo
-    rest_ref[half : half + full, :] = pack_full(cross)
-    rest_ref[half + full :, :] = from_row(f)
-
-
-def first_rest_kernel(inv_ref, xt2_ref, own_ref, other_ref, own_f_ref, other_f_ref, rest_ref, xt_ref, z_ref):
+def put_rest(rest_ref, packed, cross, f):
+    size = packed.shape[0]
+    rest_ref[:size, :] = with_rhs(packed, f)
+    rest_ref[size:, :] = pack_full(cross)
+
+
+def first_rest_kernel(inv_ref, xt2_ref, own_ref, other_ref, after_this_ref, rest_ref, xt_ref):
     half = inv_ref.shape[0]
     upper = is_upper(0)
     os1, os2 = order(upper, own_ref[:half, half:], other_ref[:half, half:])
     oo1, _ = order(upper, own_ref[:half, :half], other_ref[:half, :half])
-    less, cross, f = merge(upper, inv_ref, xt2_ref, os1, os2, own_f_ref[...], other_f_ref[...], xt_ref, z_ref)
-    put_rest(rest_ref, pack_symmetric(oo1 - less), cross, f)
+    xt = mm(os1, inv_ref[...])
+    xt_ref[:half, :] = xt
+    xt_ref[half:, :] = xt2_ref[...]
+    both = mm_nt(xt, jnp.concatenate([os1, os2], axis=0))
+    packed = pack_symmetric(oo1 - both[:, :half])
+    rest_ref[: packed.shape[0], :] = packed
+    rest_ref[packed.shape[0] :, :] = pack_full(-both[:, half:])
+
+
+def first_rhs_kernel(inv_ref, xt_ref, own_f_ref, other_f_ref, part_ref, rest_ref, z_ref):
+    half = inv_ref.shape[0]
+    size = rest_ref.shape[0] - half * 3 // 2
+    shared, outer = split_rhs(is_upper(0), own_f_ref[...], other_f_ref[...])
+    shared = jnp.broadcast_to(shared, (8, half))
+    z_ref[...] = mm(shared, inv_ref[...])[:1]
+    rest_ref[:size, :] = with_rhs(part_ref[:size, :], outer - mm_nt(shared, xt_ref[...])[:1])
+    rest_ref[size:, :] = part_ref[size:, :]
 
 
 def unpacked(upper, own_ref, other_ref, half):
-    full = half * 3 // 2
-    oo1, oo2 = order(upper, own_ref[:half, :], other_ref[:half, :])
-    os1, os2 = order(upper, own_ref[half : half + full, :], other_ref[half : half + full, :])
-    return os1, os2, oo1, oo2, own_ref[half + full :, :], other_ref[half + full :, :]
+    size = own_ref.shape[0] - half * 3 // 2
+    oo1, oo2 = order(upper, own_ref[:size, :], other_ref[:size, :])
+    os1, os2 = order(upper, own_ref[size:, :], other_ref[size:, :])
+    return os1, os2, oo1, oo2, own_ref[size - 8 : size, :], other_ref[size - 8 : size, :]
 
 
 def rest_kernel(level, inv_ref, xt2_ref, own_ref, other_ref, rest_ref, xt_ref, z_ref):
@@ -346,10 +385,8 @@
     vu = mm_nt(stacked, jnp.concatenate([g, r], axis=0))
     end_v_ref[...] = vu[:, :half]
     lost = mm_nt(vu[:, half:], vu[:half, :half])
-    t_ref[:half, :] = oo2 - pack_symmetric(work_ref[:, half:] + lost[:half])
-    t_ref[half:, :] = from_row(
-        jnp.concatenate([f[:, half:] - lost[half : half + 1], jnp.zeros((1, half), jnp.float32)], axis=1)
-    )
+    g_row = jnp.concatenate([f[:, half:] - lost[half : half + 1], jnp.zeros((1, half), jnp.float32)], axis=1)
+    t_ref[...] = with_rhs(oo2 - pack_symmetric(work_ref[:, half:] + lost[:half]), g_row)
 
 
 def compose_kernel(levels, end_v_ref, end_r_ref, *refs):
@@ -371,9 +408,9 @@
     half = map_ref.shape[0] - 8
     width = map_ref.shape[1]
     total = own_ref[...] + other_ref[...]
-    right = jnp.broadcast_to(to_row(total[half:])[:, :half], (8, half)).T
+    right = jnp.broadcast_to(to_row(total[-8:])[:, :half], (8, half)).T
     pad = jnp.zeros((half, lanes - half % lanes - 8), jnp.float32)
-    g, r = factorize(jnp.concatenate([unpack_symmetric(total[:half]), right, pad], axis=1), half // 2)
+    g, r = factorize(jnp.concatenate([unpack_symmetric(total), right, pad], axis=1), half // 2)
     shared = jnp.sum(g[:, half : half + 1] * r[:, :half], axis=0, keepdims=True)
     shared = jnp.broadcast_to(shared, (8, half)).T[:, :1]
     parts = jnp.broadcast_to(shared, (half, width)) * map_ref[:half, :]
@@ -427,8 +464,9 @@
     half = width // 2
     full = half * 3 // 2
     levels = lax.axis_size(everywhere).bit_length() - 1
-    rest_shapes = [(half + full + 8, lanes), (width, half), (1, half)]
-    shared_shapes = [(half, lanes), (half, half)]
+    packed = half * 5 // 6 + 8
+    rest_shapes = [(packed + full, lanes), (width, half), (1, half)]
+    shared_shapes = [(packed, lanes), (half, half)]
 
     schur = leaf_schur.reshape(width, width)
     other_schur = partner(schur, 0)
@@ -437,7 +475,7 @@
     ss, inverse, xt2, where = call(
         first_kernel,
         "factor_0",
-        [(half, lanes), (half, half), (half, half), (8, lanes)],
+        [*shared_shapes, (half, half), (8, lanes)],
         8.0,
         schur,
         other_schur,
@@ -458,8 +496,9 @@
         lifting.reshape(-1, rows, cells),
         *edges,
     )
-    rest, xt, z = call(
-        first_rest_kernel, "rest_0", rest_shapes, 0.05, inverse, xt2, schur, other_schur, f, partner(f, 0)
+    part, xt = call(first_rest_kernel, "rest_0", rest_shapes[:2], 1.0, inverse, xt2, schur, other_schur, f)
+    rest, z = call(
+        first_rhs_kernel, "rest_rhs_0", rest_shapes[::2], 0.05, inverse, xt, f, partner(f, 0), part
     )
     other_rest = partner(rest, 1)
     saved = [xt, z]
@@ -479,7 +518,7 @@
             end, xt, z, end_v, end_r = call(
                 functools.partial(end_kernel, level),
                 f"end_{level}",
-                [(half + 8, lanes), (width, half), (1, half), (half + 8, half), (half, half)],
+                [(packed, lanes), (width, half), (1, half), (half + 8, half), (half, half)],
                 9.5,
                 inverse,
                 *operands,

time: 68.6 us -> 67.4 us (0.983)
  waiting for transfers between devices: 8.52 us -> 6.79 us
  Pallas kernels: 42.7 us -> 43.5 us
    ppermute x9, waiting for transfers between devices: 8.51 us -> 6.78 us  [partner(): lax.ppermute(array, everywhere, [(i, i ^ 1 << level) for i in range(count)])]
    pallas_call x14 -> x15, Pallas kernels: 42.7 us -> 43.5 us  [call(): pl.pallas_call(kernel, out_shape=outs[0] if single else outs, in_specs=[v...]
  transfers between devices with their start and end apart: 12 -> 12, of which waited for: 5 -> 5; matrix products, arithmetic and copies ran while one was open for 0% -> 0% of each run, Pallas kernels for 42% -> 44%
where the time goes in v2:
time: 67.4 us; the launch traced here: 67.2 us
  Pallas kernels  43.5 us (65%)
  starting transfers between devices  15.7 us (23%)
  waiting for transfers between devices  6.79 us (10%)
  local copies, waits for them, and re-layouts  1.08 us (2%)
    pallas_call x15, Pallas kernels, call(): pl.pallas_call(kernel, out_shape=outs[0] if single else outs, in_specs=[v...  43.5 us
    ppermute x9, starting transfers between devices, partner(): lax.ppermute(array, everywhere, [(i, i ^ 1 << level) for i in range(count)])  8.37 us
    ppermute x9, waiting for transfers between devices, partner(): lax.ppermute(array, everywhere, [(i, i ^ 1 << level) for i in range(count)])  6.78 us
    ppermute x1, starting transfers between devices, halos(): after = lax.ppermute(top, 'axial', [(j, i) for i, j in up])  3.1 us
    ppermute x1, starting transfers between devices, halos(): before = lax.ppermute(bottom, 'axial', up)  2.54 us
    ppermute x1, starting transfers between devices, halos(): sides = lax.ppermute(sides, 'azim', around)  1.66 us
  transfers between devices with their start and end apart: 12, of which 5 were waited for; matrix products, arithmetic and copies ran while one was open for 0% of the time, Pallas kernels for 44%

profile of v2, /device:TPU:0, one launch (start us, length us, event | category | flops | bytes accessed | tf_op | source)
XLA Modules:
  0.0 67.2 jit_solution(582514856937036062)
XLA Ops:
  0.0 0.5 collective-permute-start
  0.5 0.0 copy-start.1
  0.5 1.0 %copy-done.1 = f32[1,64,8,256]{3,2,1,0:T(8,128)S(1)} copy-done((f32[1,64,8,256]{3,2,1,0:T(8,128)S(1)}, f32[1,64,8,256]{3,2,1,0:T(8,128)}, u32[]{:S(2)}) %copy-start.1) | copy-done | bytes 524312
  1.5 0.0 copy-start
  1.5 0.3 edges.1
  1.8 2.5 %collective-permute-start.2 = (f32[64,256]{1,0:T(8,128)S(1)}, f32[64,256]{1,0:T(8,128)S(1)}, u32[]{:S(2)}, u32[]{:S(2)}) collective-permute-start(f32[64,256]{1,0:T(8,128)S(1)} %get-tuple-element.35), channel_id=1, source_target_pairs={{0,4},{4,8},{8,12},{12,16},{16,20},{20,24},{24,28},{28,0},{1,5},{5... | collective-permute-start | bytes 196616 | tf_op jit(solution)/shard_map/ppermute | solution.py:449
  4.3 3.1 %collective-permute-start.3 = (f32[64,256]{1,0:T(8,128)S(1)}, f32[64,256]{1,0:T(8,128)S(1)}, u32[]{:S(2)}, u32[]{:S(2)}) collective-permute-start(f32[64,256]{1,0:T(8,128)S(1)} %get-tuple-element.36), channel_id=1, source_target_pairs={{4,0},{8,4},{12,8},{16,12},{20,16},{24,20},{28,24},{0,28},{5,1},{9... | collective-permute-start | bytes 196616 | tf_op jit(solution)/shard_map/ppermute | solution.py:450
  7.4 0.0 copy-start.7
  7.4 1.7 %collective-permute-start.4 = (f32[128,8]{1,0:T(8,128)S(1)}, f32[128,8]{1,0:T(8,128)S(1)}, u32[]{:S(2)}, u32[]{:S(2)}) collective-permute-start(f32[128,8]{1,0:T(8,128)S(1)} %get-tuple-element.37), channel_id=1, source_target_pairs={{0,2},{2,0},{1,3},{3,1},{4,6},{6,4},{5,7},{7,5},{8,10},{10,8},{9,1... | collective-permute-start | bytes 12296 | tf_op jit(solution)/shard_map/ppermute | solution.py:453
  9.1 0.0 collective-permute-done.other_ref
  9.1 0.0 copy-done
  9.1 0.0 copy-done.7
  9.1 0.0 copy-start.2
  9.1 0.0 copy-start.3
  9.1 0.0 copy-start.4
  9.1 0.0 copy-start.5
  9.2 5.9 %factor_0.1 = (f32[168,128]{1,0:T(8,128)S(1)}, f32[192,192]{1,0:T(8,128)S(1)}, f32[192,192]{1,0:T(8,128)S(1)}, f32[8,128]{1,0:T(8,128)S(1)}) custom-call(f32[384,384]{1,0:T(8,128)S(1)} %bitcast.9, f32[384,384]{1,0:T(8,128)S(1)} %collective-permute-done.other_ref, s32[1,6]{1,0:T(1,128)S(1)} %bitcast.17), custom_call_target="tpu_custom_call" | custom-call | flops 8000000000 | tf_op jit(solution)/shard_map/factor_0/pallas_call | solution.py:426
  15.0 0.0 copy-start.6
  15.0 0.7 %collective-permute-start.1 = (f32[168,128]{1,0:T(8,128)S(1)}, f32[168,128]{1,0:T(8,128)S(1)}, u32[]{:S(2)}, u32[]{:S(2)}) collective-permute-start(f32[168,128]{1,0:T(8,128)S(1)} %get-tuple-element.31.own_ref.after_this_ref), channel_id=1, source_target_pairs={{0,2},{1,3},{2,0},{3,1},{4,6},{5,7},{6,4},{7,5},{8,10},{9,11},{10,... | collective-permute-start | bytes 258056 | tf_op jit(solution)/shard_map/ppermute | solution.py:440
  15.7 0.0 collective-permute-done.4.sides_ref
  15.7 0.0 collective-permute-done.2.before_ref
  15.7 0.0 collective-permute-done.3.after_ref
  15.7 0.0 copy-done.2
  15.7 0.0 copy-done.3
  15.7 0.0 copy-done.4
  15.7 0.0 copy-done.5
  15.8 0.0 copy-done.6
  15.8 0.9 %leaf_rhs.1.after_this_ref.own_f_ref = f32[8,128]{1,0:T(8,128)S(1)} custom-call(f32[8,128]{1,0:T(8,128)S(1)} %get-tuple-element.34.where_ref, f32[168,128]{1,0:T(8,128)S(1)} %get-tuple-element.31.own_ref.after_this_ref, f32[64,8,256]{2,1,0:T(8,128)S(1)} %bitcast.12, f32[64,8,256]{2,1,0:T(8,128)S(1)} %bitcast.13, f32[8,256]{1,0:T(8,128)S(1)} %bitcast.16, ...), custom_call_target="tpu_custom_call" | custom-call | flops 2300000000 | tf_op jit(solution)/shard_map/leaf_rhs/pallas_call | solution.py:426
  16.7 0.0 collective-permute-start.5
  16.7 1.0 %rest_0.1 = (f32[456,128]{1,0:T(8,128)S(1)}, f32[384,192]{1,0:T(8,128)S(1)}) custom-call(f32[192,192]{1,0:T(8,128)S(1)} %get-tuple-element.32.inv_ref, f32[192,192]{1,0:T(8,128)S(1)} %get-tuple-element.33.xt2_ref, f32[384,384]{1,0:T(8,128)S(1)} %bitcast.10, f32[384,384]{1,0:T(8,128)S(1)} %collective-permute-done.other_ref, ...), custom_call_target="tpu_custom_call" | custom-call | flops 1000000000 | tf_op jit(solution)/shard_map/rest_0/pallas_call | solution.py:426
  17.7 0.1 collective-permute-done.5.other_f_ref
  17.9 0.5 rest_rhs_0.1
  18.4 1.4 %collective-permute-start.6 = (f32[456,128]{1,0:T(8,128)S(1)}, f32[456,128]{1,0:T(8,128)S(1)}, u32[]{:S(2)}, u32[]{:S(2)}) collective-permute-start(f32[456,128]{1,0:T(8,128)S(1)} %get-tuple-element.40.own_ref), channel_id=1, source_target_pairs={{0,2},{1,3},{2,0},{3,1},{4,6},{5,7},{6,4},{7,5},{8,10},{9,11},{10,... | collective-permute-start | bytes 700424 | tf_op jit(solution)/shard_map/ppermute | solution.py:440
  19.8 0.0 collective-permute-done.1.other_ref
  19.8 5.1 %factor_1.1.inv_ref = f32[192,192]{1,0:T(8,128)S(1)} custom-call(f32[168,128]{1,0:T(8,128)S(1)} %get-tuple-element.31.own_ref.after_this_ref, f32[168,128]{1,0:T(8,128)S(1)} %collective-permute-done.1.other_ref), custom_call_target="tpu_custom_call" | custom-call | flops 6499999744 | tf_op jit(solution)/shard_map/factor_1/pallas_call | solution.py:426
  24.9 1.5 %collective-permute-done.6.other_ref = f32[456,128]{1,0:T(8,128)S(1)} collective-permute-done((f32[456,128]{1,0:T(8,128)S(1)}, f32[456,128]{1,0:T(8,128)S(1)}, u32[]{:S(2)}, u32[]{:S(2)}) %collective-permute-start.6) | collective-permute-done | bytes 233504 | tf_op jit(solution)/shard_map/ppermute | solution.py:440
  26.4 0.9 %shared_1.1 = (f32[168,128]{1,0:T(8,128)S(1)}, f32[192,192]{1,0:T(8,128)S(1)}) custom-call(f32[192,192]{1,0:T(8,128)S(1)} %factor_1.1.inv_ref, f32[456,128]{1,0:T(8,128)S(1)} %get-tuple-element.40.own_ref, f32[456,128]{1,0:T(8,128)S(1)} %collective-permute-done.6.other_ref), custom_call_target="tpu_custom_call" | custom-call | flops 1500000000 | tf_op jit(solution)/shard_map/shared_1/pallas_call | solution.py:426
  27.3 0.1 collective-permute-start.7
  27.4 1.1 %rest_1.1 = (f32[456,128]{1,0:T(8,128)S(1)}, f32[384,192]{1,0:T(8,128)S(1)}, f32[1,192]{1,0:T(1,128)S(1)}) custom-call(f32[192,192]{1,0:T(8,128)S(1)} %factor_1.1.inv_ref, f32[192,192]{1,0:T(8,128)S(1)} %get-tuple-element.42.xt2_ref, f32[456,128]{1,0:T(8,128)S(1)} %get-tuple-element.40.own_ref, f32[456,128]{1,0:T(8,128)S(1)} %collective-permute-done.6.other_ref), custom_call_target="tpu_custom_call" | custom-call | flops 50000000 | tf_op jit(solution)/shard_map/rest_1/pallas_call | solution.py:426
  28.4 2.0 %collective-permute-start.8 = (f32[456,128]{1,0:T(8,128)S(1)}, f32[456,128]{1,0:T(8,128)S(1)}, u32[]{:S(2)}, u32[]{:S(2)}) collective-permute-start(f32[456,128]{1,0:T(8,128)S(1)} %get-tuple-element.43.own_ref), channel_id=1, source_target_pairs={{0,4},{1,5},{2,6},{3,7},{4,0},{5,1},{6,2},{7,3},{8,12},{9,13},{10,... | collective-permute-start | bytes 700424 | tf_op jit(solution)/shard_map/ppermute | solution.py:440
  30.5 2.3 %collective-permute-done.7.other_ref = f32[168,128]{1,0:T(8,128)S(1)} collective-permute-done((f32[168,128]{1,0:T(8,128)S(1)}, f32[168,128]{1,0:T(8,128)S(1)}, u32[]{:S(2)}, u32[]{:S(2)}) %collective-permute-start.7) | collective-permute-done | bytes 86048 | tf_op jit(solution)/shard_map/ppermute | solution.py:440
  32.8 5.2 %factor_2.1.inv_ref = f32[192,192]{1,0:T(8,128)S(1)} custom-call(f32[168,128]{1,0:T(8,128)S(1)} %get-tuple-element.41.own_ref, f32[168,128]{1,0:T(8,128)S(1)} %collective-permute-done.7.other_ref), custom_call_target="tpu_custom_call" | custom-call | flops 6499999744 | tf_op jit(solution)/shard_map/factor_2/pallas_call | solution.py:426
  38.0 0.0 collective-permute-done.8.other_ref
  38.0 0.9 %shared_2.1 = (f32[168,128]{1,0:T(8,128)S(1)}, f32[192,192]{1,0:T(8,128)S(1)}) custom-call(f32[192,192]{1,0:T(8,128)S(1)} %factor_2.1.inv_ref, f32[456,128]{1,0:T(8,128)S(1)} %get-tuple-element.43.own_ref, f32[456,128]{1,0:T(8,128)S(1)} %collective-permute-done.8.other_ref), custom_call_target="tpu_custom_call" | custom-call | flops 1500000000 | tf_op jit(solution)/shard_map/shared_2/pallas_call | solution.py:426
  39.0 0.1 collective-permute-start.9
  39.0 1.1 %rest_2.1 = (f32[456,128]{1,0:T(8,128)S(1)}, f32[384,192]{1,0:T(8,128)S(1)}, f32[1,192]{1,0:T(1,128)S(1)}) custom-call(f32[192,192]{1,0:T(8,128)S(1)} %factor_2.1.inv_ref, f32[192,192]{1,0:T(8,128)S(1)} %get-tuple-element.45.xt2_ref, f32[456,128]{1,0:T(8,128)S(1)} %get-tuple-element.43.own_ref, f32[456,128]{1,0:T(8,128)S(1)} %collective-permute-done.8.other_ref), custom_call_target="tpu_custom_call" | custom-call | flops 50000000 | tf_op jit(solution)/shard_map/rest_2/pallas_call | solution.py:426
  40.1 2.0 %collective-permute-start.10 = (f32[456,128]{1,0:T(8,128)S(1)}, f32[456,128]{1,0:T(8,128)S(1)}, u32[]{:S(2)}, u32[]{:S(2)}) collective-permute-start(f32[456,128]{1,0:T(8,128)S(1)} %get-tuple-element.46.own_ref), channel_id=1, source_target_pairs={{0,8},{1,9},{2,10},{3,11},{4,12},{5,13},{6,14},{7,15},{8,0},{9,1},... | collective-permute-start | bytes 700424 | tf_op jit(solution)/shard_map/ppermute | solution.py:440
  42.1 1.5 %collective-permute-done.9.other_ref = f32[168,128]{1,0:T(8,128)S(1)} collective-permute-done((f32[168,128]{1,0:T(8,128)S(1)}, f32[168,128]{1,0:T(8,128)S(1)}, u32[]{:S(2)}, u32[]{:S(2)}) %collective-permute-start.9) | collective-permute-done | bytes 86048 | tf_op jit(solution)/shard_map/ppermute | solution.py:440
  43.6 5.1 %factor_3.1.inv_ref = f32[192,192]{1,0:T(8,128)S(1)} custom-call(f32[168,128]{1,0:T(8,128)S(1)} %get-tuple-element.44.own_ref, f32[168,128]{1,0:T(8,128)S(1)} %collective-permute-done.9.other_ref), custom_call_target="tpu_custom_call" | custom-call | flops 6499999744 | tf_op jit(solution)/shard_map/factor_3/pallas_call | solution.py:426
  48.7 0.0 collective-permute-done.10.other_ref
  48.7 6.9 %end_3.1 = (f32[168,128]{1,0:T(8,128)S(1)}, f32[384,192]{1,0:T(8,128)S(1)}, f32[1,192]{1,0:T(1,128)S(1)}, f32[200,192]{1,0:T(8,128)S(1)}, f32[192,192]{1,0:T(8,128)S(1)}) custom-call(f32[192,192]{1,0:T(8,128)S(1)} %factor_3.1.inv_ref, f32[456,128]{1,0:T(8,128)S(1)} %get-tuple-element.46.own_ref, f32[456,128]{1,0:T(8,128)S(1)} %collective-permute-done.10.other_ref), custom_call_target="tpu_custom_call" | custom-call | flops 9500000256 | tf_op jit(solution)/shard_map/end_3/pallas_call | solution.py:426
  55.6 1.5 %collective-permute-start.11 = (f32[168,128]{1,0:T(8,128)S(1)}, f32[168,128]{1,0:T(8,128)S(1)}, u32[]{:S(2)}, u32[]{:S(2)}) collective-permute-start(f32[168,128]{1,0:T(8,128)S(1)} %get-tuple-element.47.own_ref), channel_id=1, source_target_pairs={{0,16},{1,17},{2,18},{3,19},{4,20},{5,21},{6,22},{7,23},{8,24},{9,... | collective-permute-start | bytes 258056 | tf_op jit(solution)/shard_map/ppermute | solution.py:440
  57.2 3.4 %compose.1.map_ref = f32[200,384]{1,0:T(8,128)S(1)} custom-call(f32[200,192]{1,0:T(8,128)S(1)} %get-tuple-element.48.end_v_ref, f32[192,192]{1,0:T(8,128)S(1)} %get-tuple-element.49.end_r_ref, f32[384,192]{1,0:T(8,128)S(1)} %get-tuple-element.38.xt_ref.refs_0_, f32[1,192]{1,0:T(1,128)S(1)} %get-tuple-element.50.refs_1_, ...), custom_call_target="tpu_custom_call" | custom-call | flops 3700000000 | tf_op jit(solution)/shard_map/compose/pallas_call | solution.py:426
  60.6 1.4 %collective-permute-done.11.other_ref = f32[168,128]{1,0:T(8,128)S(1)} collective-permute-done((f32[168,128]{1,0:T(8,128)S(1)}, f32[168,128]{1,0:T(8,128)S(1)}, u32[]{:S(2)}, u32[]{:S(2)}) %collective-permute-start.11) | collective-permute-done | bytes 86048 | tf_op jit(solution)/shard_map/ppermute | solution.py:440
  62.0 5.2 %solve.1 = f32[1,384]{1,0:T(1,128)} custom-call(f32[168,128]{1,0:T(8,128)S(1)} %get-tuple-element.47.own_ref, f32[168,128]{1,0:T(8,128)S(1)} %collective-permute-done.11.other_ref, f32[200,384]{1,0:T(8,128)S(1)} %compose.1.map_ref), custom_call_target="tpu_custom_call" | custom-call | flops 7000000000 | tf_op jit(solution)/shard_map/solve/pallas_call | solution.py:426
Async XLA Ops:
  0.0 9.1 %collective-permute-start = (f32[384,384]{1,0:T(8,128)}, f32[384,384]{1,0:T(8,128)S(1)}, u32[]{:S(2)}, u32[]{:S(2)}) collective-permute-start(f32[384,384]{1,0:T(8,128)} %bitcast.8), channel_id=1, source_target_pairs={{0,1},{1,0},{2,3},{3,2},{4,5},{5,4},{6,7},{7,6},{8,9},{9,8},{10,11... | collective-permute-start | bytes 1769480 | tf_op jit(solution)/shard_map/ppermute | solution.py:440
  0.5 1.0 %copy-start.1 = (f32[1,64,8,256]{3,2,1,0:T(8,128)S(1)}, f32[1,64,8,256]{3,2,1,0:T(8,128)}, u32[]{:S(2)}) copy-start(f32[1,64,8,256]{3,2,1,0:T(8,128)} %param.7) | copy-start | bytes 1572868
  1.5 7.6 %copy-start = (f32[1,1,1,384,384]{4,3,2,1,0:T(8,128)S(1)}, f32[1,1,1,384,384]{4,3,2,1,0:T(8,128)}, u32[]{:S(2)}) copy-start(f32[1,1,1,384,384]{4,3,2,1,0:T(8,128)} %param.13) | copy-start | bytes 1769476
  1.8 13.9 %collective-permute-start.2 = (f32[64,256]{1,0:T(8,128)S(1)}, f32[64,256]{1,0:T(8,128)S(1)}, u32[]{:S(2)}, u32[]{:S(2)}) collective-permute-start(f32[64,256]{1,0:T(8,128)S(1)} %get-tuple-element.35), channel_id=1, source_target_pairs={{0,4},{4,8},{8,12},{12,16},{16,20},{20,24},{24,28},{28,0},{1,5},{5... | collective-permute-start | bytes 196616 | tf_op jit(solution)/shard_map/ppermute | solution.py:449
  4.3 11.4 %collective-permute-start.3 = (f32[64,256]{1,0:T(8,128)S(1)}, f32[64,256]{1,0:T(8,128)S(1)}, u32[]{:S(2)}, u32[]{:S(2)}) collective-permute-start(f32[64,256]{1,0:T(8,128)S(1)} %get-tuple-element.36), channel_id=1, source_target_pairs={{4,0},{8,4},{12,8},{16,12},{20,16},{24,20},{28,24},{0,28},{5,1},{9... | collective-permute-start | bytes 196616 | tf_op jit(solution)/shard_map/ppermute | solution.py:450
  7.4 1.7 %copy-start.7 = (s32[1,1,1,6]{3,2,1,0:T(1,128)S(1)}, s32[1,1,1,6]{3,2,1,0:T(1,128)}, u32[]{:S(2)}) copy-start(s32[1,1,1,6]{3,2,1,0:T(1,128)} %param.12) | copy-start | bytes 76
  7.4 8.3 %collective-permute-start.4 = (f32[128,8]{1,0:T(8,128)S(1)}, f32[128,8]{1,0:T(8,128)S(1)}, u32[]{:S(2)}, u32[]{:S(2)}) collective-permute-start(f32[128,8]{1,0:T(8,128)S(1)} %get-tuple-element.37), channel_id=1, source_target_pairs={{0,2},{2,0},{1,3},{3,1},{4,6},{6,4},{5,7},{7,5},{8,10},{10,8},{9,1... | collective-permute-start | bytes 12296 | tf_op jit(solution)/shard_map/ppermute | solution.py:453
  9.1 6.6 %copy-start.2 = (f32[1,64,8,256]{3,2,1,0:T(8,128)S(1)}, f32[1,64,8,256]{3,2,1,0:T(8,128)}, u32[]{:S(2)}) copy-start(f32[1,64,8,256]{3,2,1,0:T(8,128)} %param.7) | copy-start | bytes 1572868
  9.1 6.6 %copy-start.3 = (f32[1,64,8,256]{3,2,1,0:T(8,128)S(1)}, f32[1,64,8,256]{3,2,1,0:T(8,128)}, u32[]{:S(2)}) copy-start(f32[1,64,8,256]{3,2,1,0:T(8,128)} %param.8) | copy-start | bytes 1572868
  9.1 6.6 %copy-start.4 = (f32[1,6,8,256]{3,2,1,0:T(8,128)S(1)}, f32[1,6,8,256]{3,2,1,0:T(8,128)}, u32[]{:S(2)}) copy-start(f32[1,6,8,256]{3,2,1,0:T(8,128)} %param.11) | copy-start | bytes 147460
  9.1 6.6 %copy-start.5 = (f32[1,64,64]{2,1,0:T(8,128)S(1)}, f32[1,64,64]{2,1,0:T(8,128)}, u32[]{:S(2)}) copy-start(f32[1,64,64]{2,1,0:T(8,128)} %param.10) | copy-start | bytes 49156
  15.0 0.7 %copy-start.6 = (f32[1,8,256]{2,1,0:T(8,128)S(1)}, f32[1,8,256]{2,1,0:T(8,128)}, u32[]{:S(2)}) copy-start(f32[1,8,256]{2,1,0:T(8,128)} %param.9) | copy-start | bytes 24580
  15.0 4.8 %collective-permute-start.1 = (f32[168,128]{1,0:T(8,128)S(1)}, f32[168,128]{1,0:T(8,128)S(1)}, u32[]{:S(2)}, u32[]{:S(2)}) collective-permute-start(f32[168,128]{1,0:T(8,128)S(1)} %get-tuple-element.31.own_ref.after_this_ref), channel_id=1, source_target_pairs={{0,2},{1,3},{2,0},{3,1},{4,6},{5,7},{6,4},{7,5},{8,10},{9,11},{10,... | collective-permute-start | bytes 258056 | tf_op jit(solution)/shard_map/ppermute | solution.py:440
  16.7 1.2 %collective-permute-start.5 = (f32[8,128]{1,0:T(8,128)S(1)}, f32[8,128]{1,0:T(8,128)S(1)}, u32[]{:S(2)}, u32[]{:S(2)}) collective-permute-start(f32[8,128]{1,0:T(8,128)S(1)} %leaf_rhs.1.after_this_ref.own_f_ref), channel_id=1, source_target_pairs={{0,1},{1,0},{2,3},{3,2},{4,5},{5,4},{6,7},{7,6},{8,9},{9,8},{10,11... | collective-permute-start | bytes 12296 | tf_op jit(solution)/shard_map/ppermute | solution.py:440
  18.4 8.0 %collective-permute-start.6 = (f32[456,128]{1,0:T(8,128)S(1)}, f32[456,128]{1,0:T(8,128)S(1)}, u32[]{:S(2)}, u32[]{:S(2)}) collective-permute-start(f32[456,128]{1,0:T(8,128)S(1)} %get-tuple-element.40.own_ref), channel_id=1, source_target_pairs={{0,2},{1,3},{2,0},{3,1},{4,6},{5,7},{6,4},{7,5},{8,10},{9,11},{10,... | collective-permute-start | bytes 700424 | tf_op jit(solution)/shard_map/ppermute | solution.py:440
  27.3 5.5 %collective-permute-start.7 = (f32[168,128]{1,0:T(8,128)S(1)}, f32[168,128]{1,0:T(8,128)S(1)}, u32[]{:S(2)}, u32[]{:S(2)}) collective-permute-start(f32[168,128]{1,0:T(8,128)S(1)} %get-tuple-element.41.own_ref), channel_id=1, source_target_pairs={{0,4},{1,5},{2,6},{3,7},{4,0},{5,1},{6,2},{7,3},{8,12},{9,13},{10,... | collective-permute-start | bytes 258056 | tf_op jit(solution)/shard_map/ppermute | solution.py:440
  28.4 9.6 %collective-permute-start.8 = (f32[456,128]{1,0:T(8,128)S(1)}, f32[456,128]{1,0:T(8,128)S(1)}, u32[]{:S(2)}, u32[]{:S(2)}) collective-permute-start(f32[456,128]{1,0:T(8,128)S(1)} %get-tuple-element.43.own_ref), channel_id=1, source_target_pairs={{0,4},{1,5},{2,6},{3,7},{4,0},{5,1},{6,2},{7,3},{8,12},{9,13},{10,... | collective-permute-start | bytes 700424 | tf_op jit(solution)/shard_map/ppermute | solution.py:440
  39.0 4.7 %collective-permute-start.9 = (f32[168,128]{1,0:T(8,128)S(1)}, f32[168,128]{1,0:T(8,128)S(1)}, u32[]{:S(2)}, u32[]{:S(2)}) collective-permute-start(f32[168,128]{1,0:T(8,128)S(1)} %get-tuple-element.44.own_ref), channel_id=1, source_target_pairs={{0,8},{1,9},{2,10},{3,11},{4,12},{5,13},{6,14},{7,15},{8,0},{9,1},... | collective-permute-start | bytes 258056 | tf_op jit(solution)/shard_map/ppermute | solution.py:440
  40.1 8.6 %collective-permute-start.10 = (f32[456,128]{1,0:T(8,128)S(1)}, f32[456,128]{1,0:T(8,128)S(1)}, u32[]{:S(2)}, u32[]{:S(2)}) collective-permute-start(f32[456,128]{1,0:T(8,128)S(1)} %get-tuple-element.46.own_ref), channel_id=1, source_target_pairs={{0,8},{1,9},{2,10},{3,11},{4,12},{5,13},{6,14},{7,15},{8,0},{9,1},... | collective-permute-start | bytes 700424 | tf_op jit(solution)/shard_map/ppermute | solution.py:440
  55.6 6.4 %collective-permute-start.11 = (f32[168,128]{1,0:T(8,128)S(1)}, f32[168,128]{1,0:T(8,128)S(1)}, u32[]{:S(2)}, u32[]{:S(2)}) collective-permute-start(f32[168,128]{1,0:T(8,128)S(1)} %get-tuple-element.47.own_ref), channel_id=1, source_target_pairs={{0,16},{1,17},{2,18},{3,19},{4,20},{5,21},{6,22},{7,23},{8,24},{9,... | collective-permute-start | bytes 258056 | tf_op jit(solution)/shard_map/ppermute | solution.py:440

commit v3 on v2

--- a/solution.py
+++ b/solution.py
@@ -273,11 +273,18 @@
     ss_ref[...] = pack_symmetric(oo2 - mm_nt(xt2, os2))
 
 
-def factor_kernel(own_ref, other_ref, inv_ref):
-    inv_ref[...] = mm_tn(*factorize(unpack_symmetric(own_ref[...] + other_ref[...]), inv_ref.shape[0] // 3))
-
-
-def shared_kernel(level, inv_ref, own_ref, other_ref, ss_ref, xt2_ref):
+def factor_kernel(own_ref, other_ref, *refs):
+    g_ref, r_ref = refs[-2:]
+    g_ref[...], r_ref[...] = factorize(unpack_symmetric(own_ref[...] + other_ref[...]), g_ref.shape[0] // 2)
+
+
+def inverse_kernel(g_ref, r_ref, *refs):
+    inv_ref = refs[-1]
+    inv_ref[...] = mm_tn(g_ref[...], r_ref[...])
+
+
+def shared_kernel(level, inv_ref, own_ref, other_ref, *refs):
+    ss_ref, xt2_ref = refs[-2:]
     upper = is_upper(level)
     size = ss_ref.shape[0]
     _, oo2 = order(upper, own_ref[:size, :], other_ref[:size, :])
@@ -312,7 +319,7 @@
     rest_ref[size:, :] = pack_full(cross)
 
 
-def first_rest_kernel(inv_ref, xt2_ref, own_ref, other_ref, after_this_ref, rest_ref, xt_ref):
+def first_rest_kernel(inv_ref, xt2_ref, own_ref, other_ref, rest_ref, xt_ref):
     half = inv_ref.shape[0]
     upper = is_upper(0)
     os1, os2 = order(upper, own_ref[:half, half:], other_ref[:half, half:])
@@ -326,14 +333,12 @@
     rest_ref[packed.shape[0] :, :] = pack_full(-both[:, half:])
 
 
-def first_rhs_kernel(inv_ref, xt_ref, own_f_ref, other_f_ref, part_ref, rest_ref, z_ref):
+def first_rhs_kernel(inv_ref, xt_ref, own_f_ref, other_f_ref, f_ref, z_ref):
     half = inv_ref.shape[0]
-    size = rest_ref.shape[0] - half * 3 // 2
     shared, outer = split_rhs(is_upper(0), own_f_ref[...], other_f_ref[...])
     shared = jnp.broadcast_to(shared, (8, half))
     z_ref[...] = mm(shared, inv_ref[...])[:1]
-    rest_ref[:size, :] = with_rhs(part_ref[:size, :], outer - mm_nt(shared, xt_ref[...])[:1])
-    rest_ref[size:, :] = part_ref[size:, :]
+    f_ref[...] = from_row(outer - mm_nt(shared, xt_ref[...])[:1])
 
 
 def unpacked(upper, own_ref, other_ref, half):
@@ -343,9 +348,12 @@
     return os1, os2, oo1, oo2, own_ref[size - 8 : size, :], other_ref[size - 8 : size, :]
 
 
-def rest_kernel(level, inv_ref, xt2_ref, own_ref, other_ref, rest_ref, xt_ref, z_ref):
+def rest_kernel(level, inv_ref, xt2_ref, own_ref, other_ref, *refs):
+    *sides, rest_ref, xt_ref, z_ref = refs
     upper = is_upper(level)
     os1, os2, oo1, _, own_f, other_f = unpacked(upper, own_ref, other_ref, inv_ref.shape[0])
+    if sides:
+        own_f, other_f = [side[...] for side in sides]
     less, cross, f = merge(
         upper, inv_ref, xt2_ref, unpack_full(os1), unpack_full(os2), own_f, other_f, xt_ref, z_ref
     )
@@ -482,13 +490,15 @@
         separator.reshape(1, -1),
     )
     other_ss = partner(ss, 1)
+    rest, xt = call(first_rest_kernel, "rest_0", rest_shapes[:2], 0.05, inverse, xt2, schur, other_schur)
+    other_rest = partner(rest, 1)
     f = call(
         leaf_kernel,
         "leaf_rhs",
         [(8, lanes)],
         2.3,
         where,
-        ss,
+        rest,
         state,
         adjoint_source.reshape(chans, rows, cells),
         reaction_rate.reshape(rows, cells),
@@ -496,22 +506,34 @@
         lifting.reshape(-1, rows, cells),
         *edges,
     )
-    part, xt = call(first_rest_kernel, "rest_0", rest_shapes[:2], 1.0, inverse, xt2, schur, other_schur, f)
-    rest, z = call(
-        first_rhs_kernel, "rest_rhs_0", rest_shapes[::2], 0.05, inverse, xt, f, partner(f, 0), part
+    f, z = call(
+        first_rhs_kernel, "rest_rhs_0", [(8, lanes), (1, half)], 0.5, inverse, xt, f, partner(f, 0)
     )
-    other_rest = partner(rest, 1)
+    sides = (f, partner(f, 1))
     saved = [xt, z]
     for level in range(1, levels - 1):
-        inverse = call(factor_kernel, f"factor_{level}", [(half, half)], 6.5, ss, other_ss)
+        factors = call(factor_kernel, f"factor_{level}", [(half, half), (half, half)], 5.0 if level > 1 else 0.3, ss, other_ss, *sides[:1])
+        inverse = call(inverse_kernel, f"inverse_{level}", [(half, half)], 0.5, *factors, *sides[1:])
         operands = (rest, other_rest)
         if level < levels - 2:
             ss, xt2 = call(
-                functools.partial(shared_kernel, level), f"shared_{level}", shared_shapes, 1.5, inverse, *operands
+                functools.partial(shared_kernel, level),
+                f"shared_{level}",
+                shared_shapes,
+                1.5,
+                inverse,
+                *operands,
             )
             other_ss = partner(ss, level + 1)
             rest, xt, z = call(
-                functools.partial(rest_kernel, level), f"rest_{level}", rest_shapes, 0.05, inverse, xt2, *operands
+                functools.partial(rest_kernel, level),
+                f"rest_{level}",
+                rest_shapes,
+                0.05,
+                inverse,
+                xt2,
+                *operands,
+                *sides,
             )
             other_rest = partner(rest, level + 1)
         else:
@@ -525,6 +547,7 @@
                 scratch=[(half, width)],
             )
         saved += [xt, z]
+        sides = ()
     other_end = partner(end, levels - 1)
     composed = call(
         functools.partial(compose_kernel, levels - 1), "compose", [(half + 8, width)], 3.7, end_v, end_r, *saved

time: 67.4 us -> 66.3 us (0.984)
  Pallas kernels: 43.5 us -> 42.6 us
    pallas_call x15 -> x18, Pallas kernels: 43.5 us -> 42.6 us  [call(): pl.pallas_call(kernel, out_shape=outs[0] if single else outs, in_specs=[v...]
    ppermute x9 -> x10, starting transfers between devices: 8.37 us -> 7.9 us  [partner(): lax.ppermute(array, everywhere, [(i, i ^ 1 << level) for i in range(count)])]
    ppermute x9 -> x10, waiting for transfers between devices: 6.78 us -> 7 us  [partner(): lax.ppermute(array, everywhere, [(i, i ^ 1 << level) for i in range(count)])]
  transfers between devices with their start and end apart: 12 -> 13, of which waited for: 5 -> 4; matrix products, arithmetic and copies ran while one was open for 0% -> 0% of each run, Pallas kernels for 44% -> 43%
where the time goes in v3:
time: 66.3 us; the launch traced here: 66.1 us
  Pallas kernels  42.6 us (64%)
  starting transfers between devices  15.2 us (23%)
  waiting for transfers between devices  7 us (11%)
  local copies, waits for them, and re-layouts  1.07 us (2%)
    pallas_call x18, Pallas kernels, call(): pl.pallas_call(kernel, out_shape=outs[0] if single else outs, in_specs=[v...  42.6 us
    ppermute x10, starting transfers between devices, partner(): lax.ppermute(array, everywhere, [(i, i ^ 1 << level) for i in range(count)])  7.9 us
    ppermute x10, waiting for transfers between devices, partner(): lax.ppermute(array, everywhere, [(i, i ^ 1 << level) for i in range(count)])  7 us
    ppermute x1, starting transfers between devices, halos(): after = lax.ppermute(top, 'axial', [(j, i) for i, j in up])  3.1 us
    ppermute x1, starting transfers between devices, halos(): before = lax.ppermute(bottom, 'axial', up)  2.54 us
    ppermute x1, starting transfers between devices, halos(): sides = lax.ppermute(sides, 'azim', around)  1.66 us
  transfers between devices with their start and end apart: 13, of which 4 were waited for; matrix products, arithmetic and copies ran while one was open for 0% of the time, Pallas kernels for 43%

profile of v3, /device:TPU:0, one launch (start us, length us, event | category | flops | bytes accessed | tf_op | source)
XLA Modules:
  0.0 66.1 jit_solution(12045257209348080762)
XLA Ops:
  0.0 0.5 collective-permute-start
  0.5 0.0 copy-start.1
  0.5 1.0 %copy-done.1 = f32[1,64,8,256]{3,2,1,0:T(8,128)S(1)} copy-done((f32[1,64,8,256]{3,2,1,0:T(8,128)S(1)}, f32[1,64,8,256]{3,2,1,0:T(8,128)}, u32[]{:S(2)}) %copy-start.1) | copy-done | bytes 524312
  1.5 0.0 copy-start
  1.5 0.3 edges.1
  1.8 2.5 %collective-permute-start.2 = (f32[64,256]{1,0:T(8,128)S(1)}, f32[64,256]{1,0:T(8,128)S(1)}, u32[]{:S(2)}, u32[]{:S(2)}) collective-permute-start(f32[64,256]{1,0:T(8,128)S(1)} %get-tuple-element.43), channel_id=1, source_target_pairs={{0,4},{4,8},{8,12},{12,16},{16,20},{20,24},{24,28},{28,0},{1,5},{5... | collective-permute-start | bytes 196616 | tf_op jit(solution)/shard_map/ppermute | solution.py:457
  4.3 3.1 %collective-permute-start.3 = (f32[64,256]{1,0:T(8,128)S(1)}, f32[64,256]{1,0:T(8,128)S(1)}, u32[]{:S(2)}, u32[]{:S(2)}) collective-permute-start(f32[64,256]{1,0:T(8,128)S(1)} %get-tuple-element.44), channel_id=1, source_target_pairs={{4,0},{8,4},{12,8},{16,12},{20,16},{24,20},{28,24},{0,28},{5,1},{9... | collective-permute-start | bytes 196616 | tf_op jit(solution)/shard_map/ppermute | solution.py:458
  7.4 0.0 copy-start.7
  7.4 1.7 %collective-permute-start.4 = (f32[128,8]{1,0:T(8,128)S(1)}, f32[128,8]{1,0:T(8,128)S(1)}, u32[]{:S(2)}, u32[]{:S(2)}) collective-permute-start(f32[128,8]{1,0:T(8,128)S(1)} %get-tuple-element.45), channel_id=1, source_target_pairs={{0,2},{2,0},{1,3},{3,1},{4,6},{6,4},{5,7},{7,5},{8,10},{10,8},{9,1... | collective-permute-start | bytes 12296 | tf_op jit(solution)/shard_map/ppermute | solution.py:461
  9.1 0.0 collective-permute-done.other_ref
  9.1 0.0 copy-done
  9.1 0.0 copy-done.7
  9.1 5.9 %factor_0.1 = (f32[168,128]{1,0:T(8,128)S(1)}, f32[192,192]{1,0:T(8,128)S(1)}, f32[192,192]{1,0:T(8,128)S(1)}, f32[8,128]{1,0:T(8,128)S(1)}) custom-call(f32[384,384]{1,0:T(8,128)S(1)} %bitcast.9, f32[384,384]{1,0:T(8,128)S(1)} %collective-permute-done.other_ref, s32[1,6]{1,0:T(1,128)S(1)} %bitcast.17), custom_call_target="tpu_custom_call" | custom-call | flops 8000000000 | tf_op jit(solution)/shard_map/factor_0/pallas_call | solution.py:434
  15.0 0.7 %collective-permute-start.1 = (f32[168,128]{1,0:T(8,128)S(1)}, f32[168,128]{1,0:T(8,128)S(1)}, u32[]{:S(2)}, u32[]{:S(2)}) collective-permute-start(f32[168,128]{1,0:T(8,128)S(1)} %get-tuple-element.37.own_ref), channel_id=1, source_target_pairs={{0,2},{1,3},{2,0},{3,1},{4,6},{5,7},{6,4},{7,5},{8,10},{9,11},{10,... | collective-permute-start | bytes 258056 | tf_op jit(solution)/shard_map/ppermute | solution.py:448
  15.7 0.0 copy-start.2
  15.7 0.0 copy-start.3
  15.7 0.0 copy-start.4
  15.7 0.0 copy-start.5
  15.7 1.0 %rest_0.1 = (f32[456,128]{1,0:T(8,128)S(1)}, f32[384,192]{1,0:T(8,128)S(1)}) custom-call(f32[192,192]{1,0:T(8,128)S(1)} %get-tuple-element.38.inv_ref, f32[192,192]{1,0:T(8,128)S(1)} %get-tuple-element.39.xt2_ref, f32[384,384]{1,0:T(8,128)S(1)} %bitcast.10, f32[384,384]{1,0:T(8,128)S(1)} %collective-permute-done.other_ref), custom_call_target="tpu_custom_call" | custom-call | flops 50000000 | tf_op jit(solution)/shard_map/rest_0/pallas_call | solution.py:434
  16.7 0.0 copy-start.6
  16.7 1.5 %collective-permute-start.7 = (f32[456,128]{1,0:T(8,128)S(1)}, f32[456,128]{1,0:T(8,128)S(1)}, u32[]{:S(2)}, u32[]{:S(2)}) collective-permute-start(f32[456,128]{1,0:T(8,128)S(1)} %get-tuple-element.42.after_this_ref.own_ref), channel_id=1, source_target_pairs={{0,2},{1,3},{2,0},{3,1},{4,6},{5,7},{6,4},{7,5},{8,10},{9,11},{10,... | collective-permute-start | bytes 700424 | tf_op jit(solution)/shard_map/ppermute | solution.py:448
  18.2 0.0 collective-permute-done.4.sides_ref
  18.2 0.0 collective-permute-done.2.before_ref
  18.2 0.0 collective-permute-done.3.after_ref
  18.2 0.0 copy-done.2
  18.2 0.0 copy-done.3
  18.2 0.0 copy-done.4
  18.2 0.0 copy-done.5
  18.2 0.0 copy-done.6
  18.2 0.9 %leaf_rhs.1.own_f_ref = f32[8,128]{1,0:T(8,128)S(1)} custom-call(f32[8,128]{1,0:T(8,128)S(1)} %get-tuple-element.41.where_ref, f32[456,128]{1,0:T(8,128)S(1)} %get-tuple-element.42.after_this_ref.own_ref, f32[64,8,256]{2,1,0:T(8,128)S(1)} %bitcast.12, f32[64,8,256]{2,1,0:T(8,128)S(1)} %bitcast.13, f32[8,256]{1,0:T(8,128)S(1)} %bitcast.16, ...), custom_call_target="tpu_custom_call" | custom-call | flops 2300000000 | tf_op jit(solution)/shard_map/leaf_rhs/pallas_call | solution.py:434
  19.1 0.0 collective-permute-start.5
  19.2 1.2 %collective-permute-done.5.other_f_ref = f32[8,128]{1,0:T(8,128)S(1)} collective-permute-done((f32[8,128]{1,0:T(8,128)S(1)}, f32[8,128]{1,0:T(8,128)S(1)}, u32[]{:S(2)}, u32[]{:S(2)}) %collective-permute-start.5) | collective-permute-done | bytes 4128 | tf_op jit(solution)/shard_map/ppermute | solution.py:448
  20.3 0.5 rest_rhs_0.1
  20.8 0.6 collective-permute-start.6
  21.5 0.0 collective-permute-done.1.other_ref
  21.5 4.4 %factor_1.1 = (f32[192,192]{1,0:T(8,128)S(1)}, f32[192,192]{1,0:T(8,128)S(1)}) custom-call(f32[168,128]{1,0:T(8,128)S(1)} %get-tuple-element.37.own_ref, f32[168,128]{1,0:T(8,128)S(1)} %collective-permute-done.1.other_ref, f32[8,128]{1,0:T(8,128)S(1)} %get-tuple-element.46.refs_0_), custom_call_target="tpu_custom_call" | custom-call | flops 300000000 | tf_op jit(solution)/shard_map/factor_1/pallas_call | solution.py:434
  25.9 0.0 collective-permute-done.6.refs_0_.refs_1_
  25.9 0.4 inverse_1.1.inv_ref
  26.3 0.0 collective-permute-done.7.other_ref
  26.3 0.9 %shared_1.1 = (f32[168,128]{1,0:T(8,128)S(1)}, f32[192,192]{1,0:T(8,128)S(1)}) custom-call(f32[192,192]{1,0:T(8,128)S(1)} %inverse_1.1.inv_ref, f32[456,128]{1,0:T(8,128)S(1)} %get-tuple-element.42.after_this_ref.own_ref, f32[456,128]{1,0:T(8,128)S(1)} %collective-permute-done.7.other_ref), custom_call_target="tpu_custom_call" | custom-call | flops 1500000000 | tf_op jit(solution)/shard_map/shared_1/pallas_call | solution.py:434
  27.2 0.1 collective-permute-start.8
  27.3 1.2 %rest_1.1 = (f32[456,128]{1,0:T(8,128)S(1)}, f32[384,192]{1,0:T(8,128)S(1)}, f32[1,192]{1,0:T(1,128)S(1)}) custom-call(f32[192,192]{1,0:T(8,128)S(1)} %inverse_1.1.inv_ref, f32[192,192]{1,0:T(8,128)S(1)} %get-tuple-element.52.xt2_ref, f32[456,128]{1,0:T(8,128)S(1)} %get-tuple-element.42.after_this_ref.own_ref, ...), custom_call_target="tpu_custom_call" | custom-call | flops 50000000 | tf_op jit(solution)/shard_map/rest_1/pallas_call | solution.py:434
  28.5 2.1 %collective-permute-start.9 = (f32[456,128]{1,0:T(8,128)S(1)}, f32[456,128]{1,0:T(8,128)S(1)}, u32[]{:S(2)}, u32[]{:S(2)}) collective-permute-start(f32[456,128]{1,0:T(8,128)S(1)} %get-tuple-element.53.own_ref), channel_id=1, source_target_pairs={{0,4},{1,5},{2,6},{3,7},{4,0},{5,1},{6,2},{7,3},{8,12},{9,13},{10,... | collective-permute-start | bytes 700424 | tf_op jit(solution)/shard_map/ppermute | solution.py:448
  30.6 1.9 %collective-permute-done.8.other_ref = f32[168,128]{1,0:T(8,128)S(1)} collective-permute-done((f32[168,128]{1,0:T(8,128)S(1)}, f32[168,128]{1,0:T(8,128)S(1)}, u32[]{:S(2)}, u32[]{:S(2)}) %collective-permute-start.8) | collective-permute-done | bytes 86048 | tf_op jit(solution)/shard_map/ppermute | solution.py:448
  32.5 4.4 %factor_2.1 = (f32[192,192]{1,0:T(8,128)S(1)}, f32[192,192]{1,0:T(8,128)S(1)}) custom-call(f32[168,128]{1,0:T(8,128)S(1)} %get-tuple-element.49.own_ref, f32[168,128]{1,0:T(8,128)S(1)} %collective-permute-done.8.other_ref), custom_call_target="tpu_custom_call" | custom-call | flops 5000000000 | tf_op jit(solution)/shard_map/factor_2/pallas_call | solution.py:434
  36.9 0.4 inverse_2.1.inv_ref
  37.3 0.0 collective-permute-done.9.other_ref
  37.3 0.9 %shared_2.1 = (f32[168,128]{1,0:T(8,128)S(1)}, f32[192,192]{1,0:T(8,128)S(1)}) custom-call(f32[192,192]{1,0:T(8,128)S(1)} %inverse_2.1.inv_ref, f32[456,128]{1,0:T(8,128)S(1)} %get-tuple-element.53.own_ref, f32[456,128]{1,0:T(8,128)S(1)} %collective-permute-done.9.other_ref), custom_call_target="tpu_custom_call" | custom-call | flops 1500000000 | tf_op jit(solution)/shard_map/shared_2/pallas_call | solution.py:434
  38.2 0.1 collective-permute-start.10
  38.3 1.1 %rest_2.1 = (f32[456,128]{1,0:T(8,128)S(1)}, f32[384,192]{1,0:T(8,128)S(1)}, f32[1,192]{1,0:T(1,128)S(1)}) custom-call(f32[192,192]{1,0:T(8,128)S(1)} %inverse_2.1.inv_ref, f32[192,192]{1,0:T(8,128)S(1)} %get-tuple-element.57.xt2_ref, f32[456,128]{1,0:T(8,128)S(1)} %get-tuple-element.53.own_ref, f32[456,128]{1,0:T(8,128)S(1)} %collective-permute-done.9.other_ref), custom_call_target="tpu_custom_call" | custom-call | flops 50000000 | tf_op jit(solution)/shard_map/rest_2/pallas_call | solution.py:434
  39.4 2.0 %collective-permute-start.11 = (f32[456,128]{1,0:T(8,128)S(1)}, f32[456,128]{1,0:T(8,128)S(1)}, u32[]{:S(2)}, u32[]{:S(2)}) collective-permute-start(f32[456,128]{1,0:T(8,128)S(1)} %get-tuple-element.58.own_ref), channel_id=1, source_target_pairs={{0,8},{1,9},{2,10},{3,11},{4,12},{5,13},{6,14},{7,15},{8,0},{9,1},... | collective-permute-start | bytes 700424 | tf_op jit(solution)/shard_map/ppermute | solution.py:448
  41.4 2.3 %collective-permute-done.10.other_ref = f32[168,128]{1,0:T(8,128)S(1)} collective-permute-done((f32[168,128]{1,0:T(8,128)S(1)}, f32[168,128]{1,0:T(8,128)S(1)}, u32[]{:S(2)}, u32[]{:S(2)}) %collective-permute-start.10) | collective-permute-done | bytes 86048 | tf_op jit(solution)/shard_map/ppermute | solution.py:448
  43.7 4.4 %factor_3.1 = (f32[192,192]{1,0:T(8,128)S(1)}, f32[192,192]{1,0:T(8,128)S(1)}) custom-call(f32[168,128]{1,0:T(8,128)S(1)} %get-tuple-element.54.own_ref, f32[168,128]{1,0:T(8,128)S(1)} %collective-permute-done.10.other_ref), custom_call_target="tpu_custom_call" | custom-call | flops 5000000000 | tf_op jit(solution)/shard_map/factor_3/pallas_call | solution.py:434
  48.1 0.4 inverse_3.1.inv_ref
  48.5 0.0 collective-permute-done.11.other_ref
  48.5 7.0 %end_3.1 = (f32[168,128]{1,0:T(8,128)S(1)}, f32[384,192]{1,0:T(8,128)S(1)}, f32[1,192]{1,0:T(1,128)S(1)}, f32[200,192]{1,0:T(8,128)S(1)}, f32[192,192]{1,0:T(8,128)S(1)}) custom-call(f32[192,192]{1,0:T(8,128)S(1)} %inverse_3.1.inv_ref, f32[456,128]{1,0:T(8,128)S(1)} %get-tuple-element.58.own_ref, f32[456,128]{1,0:T(8,128)S(1)} %collective-permute-done.11.other_ref), custom_call_target="tpu_custom_call" | custom-call | flops 9500000256 | tf_op jit(solution)/shard_map/end_3/pallas_call | solution.py:434
  55.5 0.4 collective-permute-start.12
  55.9 3.4 %compose.1.map_ref = f32[200,384]{1,0:T(8,128)S(1)} custom-call(f32[200,192]{1,0:T(8,128)S(1)} %get-tuple-element.60.end_v_ref, f32[192,192]{1,0:T(8,128)S(1)} %get-tuple-element.61.end_r_ref, f32[384,192]{1,0:T(8,128)S(1)} %get-tuple-element.40.xt_ref.refs_0_, f32[1,192]{1,0:T(1,128)S(1)} %get-tuple-element.62.refs_1_, ...), custom_call_target="tpu_custom_call" | custom-call | flops 3700000000 | tf_op jit(solution)/shard_map/compose/pallas_call | solution.py:434
  59.3 1.6 %collective-permute-done.12.other_ref = f32[168,128]{1,0:T(8,128)S(1)} collective-permute-done((f32[168,128]{1,0:T(8,128)S(1)}, f32[168,128]{1,0:T(8,128)S(1)}, u32[]{:S(2)}, u32[]{:S(2)}) %collective-permute-start.12) | collective-permute-done | bytes 86048 | tf_op jit(solution)/shard_map/ppermute | solution.py:448
  60.9 5.2 %solve.1 = f32[1,384]{1,0:T(1,128)} custom-call(f32[168,128]{1,0:T(8,128)S(1)} %get-tuple-element.59.own_ref, f32[168,128]{1,0:T(8,128)S(1)} %collective-permute-done.12.other_ref, f32[200,384]{1,0:T(8,128)S(1)} %compose.1.map_ref), custom_call_target="tpu_custom_call" | custom-call | flops 7000000000 | tf_op jit(solution)/shard_map/solve/pallas_call | solution.py:434
Async XLA Ops:
  0.0 9.1 %collective-permute-start = (f32[384,384]{1,0:T(8,128)}, f32[384,384]{1,0:T(8,128)S(1)}, u32[]{:S(2)}, u32[]{:S(2)}) collective-permute-start(f32[384,384]{1,0:T(8,128)} %bitcast.8), channel_id=1, source_target_pairs={{0,1},{1,0},{2,3},{3,2},{4,5},{5,4},{6,7},{7,6},{8,9},{9,8},{10,11... | collective-permute-start | bytes 1769480 | tf_op jit(solution)/shard_map/ppermute | solution.py:448
  0.5 1.0 %copy-start.1 = (f32[1,64,8,256]{3,2,1,0:T(8,128)S(1)}, f32[1,64,8,256]{3,2,1,0:T(8,128)}, u32[]{:S(2)}) copy-start(f32[1,64,8,256]{3,2,1,0:T(8,128)} %param.7) | copy-start | bytes 1572868
  1.5 7.6 %copy-start = (f32[1,1,1,384,384]{4,3,2,1,0:T(8,128)S(1)}, f32[1,1,1,384,384]{4,3,2,1,0:T(8,128)}, u32[]{:S(2)}) copy-start(f32[1,1,1,384,384]{4,3,2,1,0:T(8,128)} %param.13) | copy-start | bytes 1769476
  1.8 16.4 %collective-permute-start.2 = (f32[64,256]{1,0:T(8,128)S(1)}, f32[64,256]{1,0:T(8,128)S(1)}, u32[]{:S(2)}, u32[]{:S(2)}) collective-permute-start(f32[64,256]{1,0:T(8,128)S(1)} %get-tuple-element.43), channel_id=1, source_target_pairs={{0,4},{4,8},{8,12},{12,16},{16,20},{20,24},{24,28},{28,0},{1,5},{5... | collective-permute-start | bytes 196616 | tf_op jit(solution)/shard_map/ppermute | solution.py:457
  4.3 13.9 %collective-permute-start.3 = (f32[64,256]{1,0:T(8,128)S(1)}, f32[64,256]{1,0:T(8,128)S(1)}, u32[]{:S(2)}, u32[]{:S(2)}) collective-permute-start(f32[64,256]{1,0:T(8,128)S(1)} %get-tuple-element.44), channel_id=1, source_target_pairs={{4,0},{8,4},{12,8},{16,12},{20,16},{24,20},{28,24},{0,28},{5,1},{9... | collective-permute-start | bytes 196616 | tf_op jit(solution)/shard_map/ppermute | solution.py:458
  7.4 1.7 %copy-start.7 = (s32[1,1,1,6]{3,2,1,0:T(1,128)S(1)}, s32[1,1,1,6]{3,2,1,0:T(1,128)}, u32[]{:S(2)}) copy-start(s32[1,1,1,6]{3,2,1,0:T(1,128)} %param.12) | copy-start | bytes 76
  7.4 10.7 %collective-permute-start.4 = (f32[128,8]{1,0:T(8,128)S(1)}, f32[128,8]{1,0:T(8,128)S(1)}, u32[]{:S(2)}, u32[]{:S(2)}) collective-permute-start(f32[128,8]{1,0:T(8,128)S(1)} %get-tuple-element.45), channel_id=1, source_target_pairs={{0,2},{2,0},{1,3},{3,1},{4,6},{6,4},{5,7},{7,5},{8,10},{10,8},{9,1... | collective-permute-start | bytes 12296 | tf_op jit(solution)/shard_map/ppermute | solution.py:461
  15.0 6.5 %collective-permute-start.1 = (f32[168,128]{1,0:T(8,128)S(1)}, f32[168,128]{1,0:T(8,128)S(1)}, u32[]{:S(2)}, u32[]{:S(2)}) collective-permute-start(f32[168,128]{1,0:T(8,128)S(1)} %get-tuple-element.37.own_ref), channel_id=1, source_target_pairs={{0,2},{1,3},{2,0},{3,1},{4,6},{5,7},{6,4},{7,5},{8,10},{9,11},{10,... | collective-permute-start | bytes 258056 | tf_op jit(solution)/shard_map/ppermute | solution.py:448
  15.7 2.5 %copy-start.2 = (f32[1,64,8,256]{3,2,1,0:T(8,128)S(1)}, f32[1,64,8,256]{3,2,1,0:T(8,128)}, u32[]{:S(2)}) copy-start(f32[1,64,8,256]{3,2,1,0:T(8,128)} %param.7) | copy-start | bytes 1572868
  15.7 2.5 %copy-start.3 = (f32[1,64,8,256]{3,2,1,0:T(8,128)S(1)}, f32[1,64,8,256]{3,2,1,0:T(8,128)}, u32[]{:S(2)}) copy-start(f32[1,64,8,256]{3,2,1,0:T(8,128)} %param.8) | copy-start | bytes 1572868
  15.7 2.5 %copy-start.4 = (f32[1,6,8,256]{3,2,1,0:T(8,128)S(1)}, f32[1,6,8,256]{3,2,1,0:T(8,128)}, u32[]{:S(2)}) copy-start(f32[1,6,8,256]{3,2,1,0:T(8,128)} %param.11) | copy-start | bytes 147460
  15.7 2.5 %copy-start.5 = (f32[1,64,64]{2,1,0:T(8,128)S(1)}, f32[1,64,64]{2,1,0:T(8,128)}, u32[]{:S(2)}) copy-start(f32[1,64,64]{2,1,0:T(8,128)} %param.10) | copy-start | bytes 49156
  16.7 1.5 %copy-start.6 = (f32[1,8,256]{2,1,0:T(8,128)S(1)}, f32[1,8,256]{2,1,0:T(8,128)}, u32[]{:S(2)}) copy-start(f32[1,8,256]{2,1,0:T(8,128)} %param.9) | copy-start | bytes 24580
  16.7 9.6 %collective-permute-start.7 = (f32[456,128]{1,0:T(8,128)S(1)}, f32[456,128]{1,0:T(8,128)S(1)}, u32[]{:S(2)}, u32[]{:S(2)}) collective-permute-start(f32[456,128]{1,0:T(8,128)S(1)} %get-tuple-element.42.after_this_ref.own_ref), channel_id=1, source_target_pairs={{0,2},{1,3},{2,0},{3,1},{4,6},{5,7},{6,4},{7,5},{8,10},{9,11},{10,... | collective-permute-start | bytes 700424 | tf_op jit(solution)/shard_map/ppermute | solution.py:448
  19.1 1.2 %collective-permute-start.5 = (f32[8,128]{1,0:T(8,128)S(1)}, f32[8,128]{1,0:T(8,128)S(1)}, u32[]{:S(2)}, u32[]{:S(2)}) collective-permute-start(f32[8,128]{1,0:T(8,128)S(1)} %leaf_rhs.1.own_f_ref), channel_id=1, source_target_pairs={{0,1},{1,0},{2,3},{3,2},{4,5},{5,4},{6,7},{7,6},{8,9},{9,8},{10,11... | collective-permute-start | bytes 12296 | tf_op jit(solution)/shard_map/ppermute | solution.py:448
  20.8 5.1 %collective-permute-start.6 = (f32[8,128]{1,0:T(8,128)S(1)}, f32[8,128]{1,0:T(8,128)S(1)}, u32[]{:S(2)}, u32[]{:S(2)}) collective-permute-start(f32[8,128]{1,0:T(8,128)S(1)} %get-tuple-element.46.refs_0_), channel_id=1, source_target_pairs={{0,2},{1,3},{2,0},{3,1},{4,6},{5,7},{6,4},{7,5},{8,10},{9,11},{10,... | collective-permute-start | bytes 12296 | tf_op jit(solution)/shard_map/ppermute | solution.py:448
  27.2 5.3 %collective-permute-start.8 = (f32[168,128]{1,0:T(8,128)S(1)}, f32[168,128]{1,0:T(8,128)S(1)}, u32[]{:S(2)}, u32[]{:S(2)}) collective-permute-start(f32[168,128]{1,0:T(8,128)S(1)} %get-tuple-element.49.own_ref), channel_id=1, source_target_pairs={{0,4},{1,5},{2,6},{3,7},{4,0},{5,1},{6,2},{7,3},{8,12},{9,13},{10,... | collective-permute-start | bytes 258056 | tf_op jit(solution)/shard_map/ppermute | solution.py:448
  28.5 8.8 %collective-permute-start.9 = (f32[456,128]{1,0:T(8,128)S(1)}, f32[456,128]{1,0:T(8,128)S(1)}, u32[]{:S(2)}, u32[]{:S(2)}) collective-permute-start(f32[456,128]{1,0:T(8,128)S(1)} %get-tuple-element.53.own_ref), channel_id=1, source_target_pairs={{0,4},{1,5},{2,6},{3,7},{4,0},{5,1},{6,2},{7,3},{8,12},{9,13},{10,... | collective-permute-start | bytes 700424 | tf_op jit(solution)/shard_map/ppermute | solution.py:448
  38.2 5.5 %collective-permute-start.10 = (f32[168,128]{1,0:T(8,128)S(1)}, f32[168,128]{1,0:T(8,128)S(1)}, u32[]{:S(2)}, u32[]{:S(2)}) collective-permute-start(f32[168,128]{1,0:T(8,128)S(1)} %get-tuple-element.54.own_ref), channel_id=1, source_target_pairs={{0,8},{1,9},{2,10},{3,11},{4,12},{5,13},{6,14},{7,15},{8,0},{9,1},... | collective-permute-start | bytes 258056 | tf_op jit(solution)/shard_map/ppermute | solution.py:448
  39.4 9.1 %collective-permute-start.11 = (f32[456,128]{1,0:T(8,128)S(1)}, f32[456,128]{1,0:T(8,128)S(1)}, u32[]{:S(2)}, u32[]{:S(2)}) collective-permute-start(f32[456,128]{1,0:T(8,128)S(1)} %get-tuple-element.58.own_ref), channel_id=1, source_target_pairs={{0,8},{1,9},{2,10},{3,11},{4,12},{5,13},{6,14},{7,15},{8,0},{9,1},... | collective-permute-start | bytes 700424 | tf_op jit(solution)/shard_map/ppermute | solution.py:448
  55.5 5.4 %collective-permute-start.12 = (f32[168,128]{1,0:T(8,128)S(1)}, f32[168,128]{1,0:T(8,128)S(1)}, u32[]{:S(2)}, u32[]{:S(2)}) collective-permute-start(f32[168,128]{1,0:T(8,128)S(1)} %get-tuple-element.59.own_ref), channel_id=1, source_target_pairs={{0,16},{1,17},{2,18},{3,19},{4,20},{5,21},{6,22},{7,23},{8,24},{9,... | collective-permute-start | bytes 258056 | tf_op jit(solution)/shard_map/ppermute | solution.py:448
